TPU v7x, 32 devices: a whole 2x2x4 slice. The times are simulated.
32 devices in a mesh: group: 2 (over y), ctx: 4 (over z), feat: 2 (over x), ex: 2 (over core).
Axes of the slice: x: 2, y: 2, z: 4, core: 2. Of those that a mesh axis runs over, the one named last changes fastest.
Arguments:
- hidden: bfloat16 [8, 512, 8192], P(('group', 'feat', 'ex'), 'ctx'), parts along dimension 0, may hold values from -6 to 6
- cotangent: bfloat16 [8, 512, 1024], P(('group', 'feat', 'ex'), 'ctx'), parts along dimension 0, may hold values from -6 to 6
- adapter_down_factor: bfloat16 [8192, 16], replicated, may hold values from -0.0625 to 0.0625
- projection: bfloat16 [16384, 8192], P('ctx', 'feat'), may hold values from -6 to 6
- lengths: int32 [8], P(('group', 'feat', 'ex')), parts along dimension 0, may hold values from 128 to 512, as said below
- slot_example_order: int32 [8], P('group'), parts along dimension 0, may hold values from 0 to 3, each once
Outputs:
- features: float32 [8, 8192], P(('group', 'ex'), 'feat'), parts along dimension 0
There are 2 independent parts, one for each index of `group`. A program takes and returns all parts, laid end to end along the dimension named above; an argument that names none is the same for every part. Nothing has to cross between parts.
Inputs may be any that keep to these rules, and one draw needn't show every extreme that they name: `lengths`: some example has exactly 512 valid positions and some exactly one quarter of 512.
All inputs are finite; a program needn't handle non-finite values.
Results may differ from a plain program's by a relative error of at most 0.0042.
Values may be sent and summed in bfloat16 or wider, within the bound.
A program may use at most 64 MiB of HBM per device.

v0:
```python
import jax
import jax.numpy as jnp
from jax import lax
from jax.sharding import PartitionSpec as P

FEATS = 8192


def per_device(hidden, cotangent, adapter_down_factor, projection, lengths, slot_example_order):
    ctx_count = lax.axis_size("ctx")
    feat_count = lax.axis_size("feat")
    example_groups = lax.axis_size("ex")
    example_count, token_count, model_width = hidden.shape
    down_factor_rows = jnp.dot(
        hidden.reshape(example_count * token_count, model_width),
        adapter_down_factor,
        preferred_element_type=jnp.float32,
    )
    down_factor_rows = down_factor_rows.astype(jnp.bfloat16).reshape(example_count, token_count, -1)
    position = lax.axis_index("ctx") * token_count + lax.iota(jnp.int32, token_count)
    retain_mask = (position[None, :] < lengths[:, None]).astype(jnp.bfloat16)
    down_factor_rows = down_factor_rows * retain_mask[:, :, None]
    partial_value = jnp.einsum(
        "etr,etj->erj", down_factor_rows, cotangent, preferred_element_type=jnp.float32
    )
    partial_value = partial_value.reshape(example_count, -1)
    block_size = partial_value.shape[1] // ctx_count
    summed_all = lax.psum(partial_value, "ctx")
    owned_rows = lax.dynamic_slice_in_dim(
        summed_all, lax.axis_index("ctx") * block_size, block_size, 1
    )
    grad_rows = owned_rows.astype(jnp.bfloat16)
    projected = jnp.dot(
        lax.all_gather(grad_rows, "feat", axis=0, tiled=True),
        projection,
        preferred_element_type=jnp.float32,
    )
    summed = lax.psum(projected, "ctx")
    squares = lax.psum(jnp.sum(summed * summed, axis=1), "feat")
    scaled = summed / jnp.sqrt(squares / FEATS + 1e-06)[:, None]
    everything = lax.all_gather(scaled, "ex", axis=0, tiled=True)
    arranged = jnp.transpose(
        slot_example_order.reshape(feat_count, example_groups, example_count), (1, 0, 2)
    ).reshape(-1)
    own_rows = everything.shape[0] // example_groups
    wanted = lax.axis_index("ex") * own_rows + lax.iota(jnp.int32, own_rows)
    select = (arranged[None, :] == wanted[:, None]).astype(jnp.float32)
    return jnp.dot(
        select, everything, precision=lax.Precision.HIGHEST, preferred_element_type=jnp.float32
    )


def solution(mesh):
    in_specs = (
        P(("group", "feat", "ex"), "ctx", None),
        P(("group", "feat", "ex"), "ctx", None),
        P(),
        P("ctx", "feat"),
        P(("group", "feat", "ex")),
        P("group"),
    )
    out_specs = P(("group", "ex"), "feat")
    return jax.shard_map(
        per_device, mesh=mesh, in_specs=in_specs, out_specs=out_specs, check_vma=False
    )
```

profile of v0, /device:TPU:0, one launch (start us, length us, event | category | flops | bytes accessed | tf_op | source)
XLA Modules:
  0.0 76.8 jit_solution(9681998552901455173)
XLA Ops:
  0.0 0.0 copy-start
  0.8 0.8 %copy-done = bf16[1,128,8192]{2,1,0:T(8,128)(2,1)S(1)} copy-done((bf16[1,128,8192]{2,1,0:T(8,128)(2,1)S(1)}, bf16[1,128,8192]{2,1,0:T(8,128)(2,1)}, u32[]{:S(2)}) %copy-start) | copy-done | bytes 2097176
  1.6 1.9 %convolution_bitcast_fusion = f32[1,1,16,1024]{3,2,1,0:T(8,128)S(1)} fusion(bf16[8192,16]{0,1:T(8,128)(2,1)} %param.8, bf16[1,128,8192]{2,1,0:T(8,128)(2,1)S(1)} %copy-done, bf16[1,128,1024]{2,1,0:T(8,128)(2,1)} %param.7, bf16[128]{0:T(256)(128)(2,1)S(1)} %compare_convert_fusion), kind=kOutput, calls=%fused_computation.2 | convolution fusion | flops 37752832 | bytes 2687232 | tf_op jit(solution)/shard_map/etr,etj->erj/dot_general | solution.py:23
  3.5 0.1 copy.11
  3.6 31.9 %psum.21 = bf16[1,16384]{1,0:T(2,128)(2,1)S(1)} all-reduce(f32[1,16384]{1,0:T(1,128)S(1)} %bitcast.31), channel_id=1, replica_groups=mesh['group'=2,'ctx'=4,'feat'=2,'ex'=2] {'ctx'}, use_global_device_ids=true, to_apply=%region_0.0 | all-reduce | flops 16384 | bytes 98304 | tf_op jit(solution)/shard_map/psum | solution.py:28
  35.6 4.4 %all-gather = bf16[2,1,4096]{2,1,0:T(2,128)(2,1)S(1)} all-gather(bf16[1,1,4096]{2,1,0:T(2,128)(2,1)S(1)} %convert_bitcast_fusion), channel_id=1, replica_groups=mesh['group'=2,'ctx'=4,'feat'=2,'ex'=2] {'feat'}, dimensions={0}, use_global_device_ids=true | all-gather | bytes 24576 | tf_op jit(solution)/shard_map/all_gather | solution.py:34
  40.0 0.0 copy-start.1
  40.0 12.8 %fusion.11 = f32[2,4096]{1,0:T(2,128)S(1)} fusion(bf16[4096,4096]{1,0:T(8,128)(2,1)} %param.9, bf16[2,1,4096]{2,1,0:T(2,128)(2,1)S(1)} %all-gather), kind=kOutput, calls=%fused_computation.8 | convolution fusion | flops 67108864 | bytes 33603584 | tf_op jit(solution)/shard_map/dot_general | solution.py:33
  52.8 15.8 %psum.22 = f32[2,4096]{1,0:T(2,128)S(1)} all-reduce(f32[2,4096]{1,0:T(2,128)S(1)} %fusion.11), channel_id=1, replica_groups=mesh['group'=2,'ctx'=4,'feat'=2,'ex'=2] {'ctx'}, use_global_device_ids=true, to_apply=%region_1.0 | all-reduce | flops 8192 | bytes 65536 | tf_op jit(solution)/shard_map/psum | solution.py:38
  68.6 0.1 multiply_reduce_fusion
  68.7 4.9 %psum.23 = f32[2]{0:T(128)S(1)} all-reduce(f32[2]{0:T(128)S(1)} %multiply_reduce_fusion), channel_id=1, replica_groups=mesh['group'=2,'ctx'=4,'feat'=2,'ex'=2] {'feat'}, use_global_device_ids=true, to_apply=%region_3.0 | all-reduce | flops 2 | bytes 16 | tf_op jit(solution)/shard_map/psum | solution.py:39
  73.7 0.1 divide_bitcast_fusion
  73.8 1.9 %all-gather.1 = f32[2,2,4096]{2,1,0:T(2,128)S(1)} all-gather(f32[1,2,4096]{2,1,0:T(2,128)S(1)} %divide_bitcast_fusion), channel_id=1, replica_groups=mesh['group'=2,'ctx'=4,'feat'=2,'ex'=2] {'ex'}, dimensions={0}, use_global_device_ids=true | all-gather | bytes 98304 | tf_op jit(solution)/shard_map/all_gather | solution.py:41
  75.6 0.1 reshape.45
  75.7 0.0 copy-done.1
  75.7 0.1 reshape.38
  75.8 0.1 copy.9
  75.9 0.1 eq.15
  76.0 0.9 %fusion.15 = f32[2,4096]{1,0:T(2,128)} fusion(f32[4,4096]{1,0:T(4,128)S(1)} %reshape.45, s32[4]{0:T(128)S(1)} %eq.15, s32[2]{0:T(128)S(1)} %iota_add_fusion), kind=kOutput, calls=%fused_computation.14 | convolution fusion | flops 393224 | bytes 98328 | tf_op jit(solution)/shard_map/dot_general | solution.py:48
  (4 shorter events, 0.0 us)
Async XLA Ops:
  0.0 1.6 %copy-start = (bf16[1,128,8192]{2,1,0:T(8,128)(2,1)S(1)}, bf16[1,128,8192]{2,1,0:T(8,128)(2,1)}, u32[]{:S(2)}) copy-start(bf16[1,128,8192]{2,1,0:T(8,128)(2,1)} %param.6) | copy-start | bytes 6291460
  40.0 35.7 %copy-start.1 = (s32[4]{0:T(128)S(1)}, s32[4]{0:T(128)}, u32[]{:S(2)}) copy-start(s32[4]{0:T(128)} %param.11) | copy-start | bytes 52
where the time goes:
time: 77.1 us; the launch traced here: 76.8 us
  blocking collectives  58.9 us (76%)
  matrix products  15.6 us (20%)
  local copies, waits for them, and re-layouts  1.22 us (2%)
  between operations  0.88 us (1%)
    psum x1, blocking collectives, per_device(): summed_all = lax.psum(partial_value, 'ctx')  31.9 us
    psum x1, blocking collectives, per_device(): summed = lax.psum(projected, 'ctx')  15.8 us
    dot_general x1, matrix products, per_device(): jnp.dot(lax.all_gather(grad_rows, 'feat', axis=0, tiled=True), projection...  12.8 us
    psum x1, blocking collectives, per_device(): squares = lax.psum(jnp.sum(summed * summed, axis=1), 'feat')  4.93 us
    all_gather x1, blocking collectives, per_device(): lax.all_gather(grad_rows, 'feat', axis=0, tiled=True)  4.42 us
    dot_general x1, matrix products, per_device(): jnp.einsum('etr,etj->erj', down_factor_rows, cotangent, preferred_element...  1.87 us
    all_gather x1, blocking collectives, per_device(): everything = lax.all_gather(scaled, 'ex', axis=0, tiled=True)  1.85 us

commit v1 on v0

v1 whole, which is shorter than its diff:
```python
import functools

import jax
import jax.numpy as jnp
from jax import lax
from jax.experimental import pallas as pl
from jax.experimental.pallas import tpu as pltpu
from jax.sharding import PartitionSpec as P

MESH = pl.DeviceIdType.MESH
F32 = jnp.float32
BF16 = jnp.bfloat16
FEATS = 8192
LANES = 128
HIDDEN_CHUNKS = 4


def loop(low, high, body):
    if high - low <= 4:
        for step in range(low, high):
            body(step)
    else:
        lax.fori_loop(low, high, lambda step, carry: (body(step), carry)[1], 0)


def kernel(
    sizes,
    lengths_ref, order_ref, hidden_ref, cotangent_ref, factor_ref, projection_ref,
    out_ref,
    hidden_v, cotangent_v, factor_v, projection_v,
    partial, partial_in, grads, grad_rows, rows_out, rows_in, final_out, final_in, squares_in,
    local_sem, projection_sem,
    grad_send, grad_recv, gather_send, gather_recv, rows_send, rows_recv,
    final_send, final_recv, squares_send, squares_recv,
):
    ctx_count, feat_count, ex_count = sizes
    ctx, feat, ex = lax.axis_index("ctx"), lax.axis_index("feat"), lax.axis_index("ex")
    slots = feat_count * ex_count
    slot = feat * ex_count + ex
    token_count, model_width = hidden_v.shape
    rank = factor_v.shape[0]
    own_rank = rank // ctx_count
    chunk_count, depth, chunk = projection_v.shape
    width = chunk_count * chunk
    value_width = cotangent_v.shape[1]
    padded = max(8, slots)
    own_ids = out_ref.shape[0]

    step = model_width // HIDDEN_CHUNKS
    factor_copy = pltpu.make_async_copy(factor_ref, factor_v, local_sem.at[0])
    factor_copy.start()
    hidden_copies = []
    for k in range(HIDDEN_CHUNKS):
        columns = pl.ds(k * step, step)
        hidden_copies.append(
            pltpu.make_async_copy(
                hidden_ref.at[0, :, columns], hidden_v.at[:, columns], local_sem.at[2 + k]
            )
        )
        hidden_copies[-1].start()
    cotangent_copy = pltpu.make_async_copy(cotangent_ref.at[0], cotangent_v, local_sem.at[1])
    cotangent_copy.start()
    projection_copies = []
    for k in range(chunk_count):
        columns = pl.ds(pl.multiple_of(ex * width + k * chunk, LANES), chunk)
        projection_copies.append(
            pltpu.make_async_copy(
                projection_ref.at[:, columns], projection_v.at[k], projection_sem.at[k]
            )
        )
        projection_copies[-1].start()

    barrier = pltpu.get_barrier_semaphore()
    members = ctx_count * slots
    me = ctx * slots + slot

    def greet(d):
        other = lax.rem(me + d, members)
        pl.semaphore_signal(
            barrier, inc=1, device_id_type=MESH,
            device_id={
                "ctx": other // slots,
                "feat": lax.rem(other // ex_count, feat_count),
                "ex": lax.rem(other, ex_count),
            },
        )

    loop(1, members, greet)

    pick_shape = (own_rank * padded, slots * own_rank)
    row, column = lax.broadcasted_iota(jnp.int32, pick_shape, 0), lax.broadcasted_iota(jnp.int32, pick_shape, 1)
    column_id = jnp.zeros(pick_shape, jnp.int32)
    for s in range(slots):
        column_id = jnp.where(column // own_rank == s, order_ref[s], column_id)
    pick = (row // padded == lax.rem(column, own_rank)) & (lax.rem(row, padded) == column_id)
    pick = pick.astype(F32).astype(BF16)

    factor_copy.wait()
    down = jnp.zeros((rank, token_count), F32)
    for k in range(HIDDEN_CHUNKS):
        hidden_copies[k].wait()
        columns = pl.ds(k * step, step)
        down += lax.dot_general(
            factor_v[:, columns], hidden_v[:, columns], (((1,), (1,)), ((), ())),
            preferred_element_type=F32,
        )
    position = ctx * token_count + lax.broadcasted_iota(jnp.int32, down.shape, 1)
    down = jnp.where(position < lengths_ref[0], down, 0.0).astype(BF16)
    cotangent_copy.wait()
    grad = jnp.dot(down, cotangent_v[...], preferred_element_type=F32)
    for k in range(ctx_count):
        partial[k] = grad[k * own_rank:(k + 1) * own_rank]

    pl.semaphore_wait(barrier, members - 1)

    def grad_copy(d):
        other = lax.rem(ctx + d, ctx_count)
        return pltpu.make_async_remote_copy(
            src_ref=partial.at[other], dst_ref=partial_in.at[ctx],
            send_sem=grad_send.at[d], recv_sem=grad_recv.at[ctx],
            device_id={"ctx": other}, device_id_type=MESH,
        )

    def grad_arrival(d):
        other = lax.rem(ctx + d, ctx_count)
        pltpu.make_async_remote_copy(
            src_ref=partial.at[other], dst_ref=partial_in.at[other],
            send_sem=grad_send.at[d], recv_sem=grad_recv.at[other],
            device_id={"ctx": other}, device_id_type=MESH,
        ).wait_recv()

    loop(1, ctx_count, lambda d: grad_copy(d).start())
    partial_in[ctx] = partial[ctx]
    loop(1, ctx_count, grad_arrival)
    total = partial_in[0]
    for k in range(1, ctx_count):
        total += partial_in[k]
    grads[slot] = total.astype(BF16).astype(F32)

    def gather_copy(d):
        other = lax.rem(slot + d, slots)
        return pltpu.make_async_remote_copy(
            src_ref=grads.at[slot], dst_ref=grads.at[slot],
            send_sem=gather_send.at[d], recv_sem=gather_recv.at[slot],
            device_id={"feat": other // ex_count, "ex": lax.rem(other, ex_count)},
            device_id_type=MESH,
        )

    def gather_arrival(d):
        other = lax.rem(slot + d, slots)
        pltpu.make_async_remote_copy(
            src_ref=grads.at[other], dst_ref=grads.at[other],
            send_sem=gather_send.at[d], recv_sem=gather_recv.at[other],
            device_id={"feat": other // ex_count, "ex": lax.rem(other, ex_count)},
            device_id_type=MESH,
        ).wait_recv()

    loop(1, slots, lambda d: gather_copy(d).start())
    loop(1, slots, gather_arrival)
    for s in range(slots):
        grad_rows[s * own_rank:(s + 1) * own_rank] = grads[s]
    picked = jnp.dot(pick, grad_rows[...].astype(BF16), preferred_element_type=F32)
    left = [picked[r * padded:(r + 1) * padded].astype(BF16) for r in range(own_rank)]

    for k in range(chunk_count):
        projection_copies[k].wait()
        product = jnp.zeros((padded, chunk), F32)
        for r in range(own_rank):
            product += jnp.dot(
                left[r], projection_v[k, r * value_width:(r + 1) * value_width, :],
                preferred_element_type=F32,
            )
        for i in range(slots):
            rows_out[i, :, k * chunk:(k + 1) * chunk] = product[i:i + 1]

    def rows_copy(d):
        other = lax.rem(ctx + d, ctx_count)
        return pltpu.make_async_remote_copy(
            src_ref=rows_out.at[other], dst_ref=rows_in.at[ctx],
            send_sem=rows_send.at[d], recv_sem=rows_recv.at[ctx],
            device_id={"ctx": other}, device_id_type=MESH,
        )

    def rows_arrival(d):
        other = lax.rem(ctx + d, ctx_count)
        pltpu.make_async_remote_copy(
            src_ref=rows_out.at[other], dst_ref=rows_in.at[other],
            send_sem=rows_send.at[d], recv_sem=rows_recv.at[other],
            device_id={"ctx": other}, device_id_type=MESH,
        ).wait_recv()

    loop(1, ctx_count, lambda d: rows_copy(d).start())
    rows_in[ctx] = rows_out[ctx]
    loop(1, ctx_count, rows_arrival)
    summed = rows_in[0]
    for k in range(1, ctx_count):
        summed += rows_in[k]
    square = jnp.sum(summed * summed, axis=1, keepdims=True)
    final_out[:, :width] = summed
    final_out[:, width:] = jnp.broadcast_to(square, (1, LANES))

    owner_ex = ctx // own_ids
    place = lax.rem(ctx, own_ids)
    tail = pl.ds(width, LANES)

    def final_copy(d):
        return pltpu.make_async_remote_copy(
            src_ref=final_out, dst_ref=final_in.at[place * ex_count + ex],
            send_sem=final_send.at[d], recv_sem=final_recv.at[place * ex_count + ex],
            device_id={"ctx": lax.rem(ctx + d, ctx_count), "ex": owner_ex},
            device_id_type=MESH,
        )

    def squares_copy(q):
        d, g = q // (feat_count - 1), lax.rem(q, feat_count - 1) + 1
        return pltpu.make_async_remote_copy(
            src_ref=final_out.at[:, tail],
            dst_ref=squares_in.at[feat, place * ex_count + ex],
            send_sem=squares_send.at[q], recv_sem=squares_recv.at[feat, place * ex_count + ex],
            device_id={
                "ctx": lax.rem(ctx + d, ctx_count),
                "feat": lax.rem(feat + g, feat_count),
                "ex": owner_ex,
            },
            device_id_type=MESH,
        )

    def final_arrival(q):
        pltpu.make_async_remote_copy(
            src_ref=final_out, dst_ref=final_in.at[q],
            send_sem=final_send.at[0], recv_sem=final_recv.at[q],
            device_id={"ctx": lax.rem(ctx + 1, ctx_count)}, device_id_type=MESH,
        ).wait_recv()

    def squares_arrival(q):
        g, source = q // (own_ids * ex_count) + 1, lax.rem(q, own_ids * ex_count)
        other = lax.rem(feat + g, feat_count)
        pltpu.make_async_remote_copy(
            src_ref=final_out.at[:, tail], dst_ref=squares_in.at[other, source],
            send_sem=squares_send.at[0], recv_sem=squares_recv.at[other, source],
            device_id={"feat": other}, device_id_type=MESH,
        ).wait_recv()

    square_sends = ctx_count * (feat_count - 1)
    owner = owner_ex == ex
    mine = place * ex_count + ex
    loop(0, square_sends, lambda q: squares_copy(q).start())
    loop(1, ctx_count, lambda d: final_copy(d).start())

    @pl.when(jnp.logical_not(owner))
    def _():
        final_copy(0).start()

    @pl.when(owner)
    def _():
        final_in[mine] = final_out[...]

    def arrive(q):
        @pl.when(jnp.logical_not(owner & (mine == q)))
        def _():
            final_arrival(q)

    loop(0, own_ids * ex_count, arrive)
    loop(0, (feat_count - 1) * own_ids * ex_count, squares_arrival)
    squares_in[feat] = final_in[:, :, width:]
    for i in range(own_ids):
        everything = squares_in[0, i * ex_count]
        for q in range(1, feat_count * ex_count):
            everything += squares_in[q // ex_count, i * ex_count + q % ex_count]
        norm = jnp.sqrt(everything[:, :1] / FEATS + 1e-06)
        for k in range(ex_count):
            out_ref[i:i + 1, k * width:(k + 1) * width] = final_in[i * ex_count + k, :, :width] / norm

    loop(1, ctx_count, lambda d: grad_copy(d).wait_send())
    loop(1, slots, lambda d: gather_copy(d).wait_send())
    loop(1, ctx_count, lambda d: rows_copy(d).wait_send())
    loop(1, ctx_count, lambda d: final_copy(d).wait_send())
    loop(0, square_sends, lambda q: squares_copy(q).wait_send())

    @pl.when(jnp.logical_not(owner))
    def _():
        final_copy(0).wait_send()


def per_device(sizes, hidden, cotangent, adapter_down_factor, projection, lengths, slot_example_order):
    ctx_count, feat_count, ex_count = sizes
    slots = feat_count * ex_count
    example_count, token_count, model_width = hidden.shape
    value_width = cotangent.shape[2]
    rank = adapter_down_factor.shape[1]
    depth, columns = projection.shape
    width = columns // ex_count
    chunk = min(512, width)
    own_ids = slots // ex_count
    own_rank = rank // ctx_count
    assert example_count == 1 and slots == ctx_count
    assert depth == own_rank * value_width
    dma = pltpu.SemaphoreType.DMA
    return pl.pallas_call(
        functools.partial(kernel, sizes),
        out_shape=jax.ShapeDtypeStruct((own_ids, columns), F32),
        in_specs=[pl.BlockSpec(memory_space=pltpu.SMEM)] * 2 + [pl.BlockSpec(memory_space=pl.ANY)] * 4,
        out_specs=pl.BlockSpec(memory_space=pltpu.VMEM),
        scratch_shapes=[
            pltpu.VMEM((token_count, model_width), BF16),
            pltpu.VMEM((token_count, value_width), BF16),
            pltpu.VMEM((rank, model_width), BF16),
            pltpu.VMEM((width // chunk, depth, chunk), BF16),
            pltpu.VMEM((ctx_count, own_rank, value_width), F32),
            pltpu.VMEM((ctx_count, own_rank, value_width), F32),
            pltpu.VMEM((slots, own_rank, value_width), F32),
            pltpu.VMEM((slots * own_rank, value_width), F32),
            pltpu.VMEM((slots, 1, width), F32),
            pltpu.VMEM((ctx_count, 1, width), F32),
            pltpu.VMEM((1, width + LANES), F32),
            pltpu.VMEM((own_ids * ex_count, 1, width + LANES), F32),
            pltpu.VMEM((feat_count, own_ids * ex_count, 1, LANES), F32),
            dma((2 + HIDDEN_CHUNKS,)),
            dma((width // chunk,)),
            dma((ctx_count,)),
            dma((ctx_count,)),
            dma((slots,)),
            dma((slots,)),
            dma((ctx_count,)),
            dma((ctx_count,)),
            dma((ctx_count,)),
            dma((own_ids * ex_count,)),
            dma((ctx_count * (feat_count - 1),)),
            dma((feat_count, own_ids * ex_count)),
        ],
        compiler_params=pltpu.CompilerParams(
            collective_id=0, has_side_effects=True, vmem_limit_bytes=48 * 1024 * 1024
        ),
    )(lengths, slot_example_order, hidden, cotangent, adapter_down_factor.T, projection)


def solution(mesh):
    in_specs = (
        P(("group", "feat", "ex"), "ctx", None),
        P(("group", "feat", "ex"), "ctx", None),
        P(),
        P("ctx", "feat"),
        P(("group", "feat", "ex")),
        P("group"),
    )
    out_specs = P(("group", "ex"), "feat")
    sizes = (mesh.shape["ctx"], mesh.shape["feat"], mesh.shape["ex"])
    return jax.shard_map(
        functools.partial(per_device, sizes),
        mesh=mesh, in_specs=in_specs, out_specs=out_specs, check_vma=False,
    )
```

time: 77.1 us -> 29.3 us (0.38)
  blocking collectives: 58.9 us -> 0 us
  Pallas kernels: 0 us -> 23.7 us
  matrix products: 15.6 us -> 0 us
  local copies, waits for them, and re-layouts: 1.22 us -> 4.76 us
    psum x3 -> x0, blocking collectives: 52.6 us -> none  [the longest x1 31.9 us: per_device(): summed_all = lax.psum(partial_value, 'ctx')]
    pallas_call x0 -> x1, Pallas kernels: none -> 23.7 us  [per_device(): pl.pallas_call(functools.partial(kernel, sizes), out_shape=jax.ShapeDtype...]
    dot_general x3 -> x0, matrix products: 15.6 us -> none  [the longest x1 12.8 us: per_device(): jnp.dot(lax.all_gather(grad_rows, 'feat', axis=0, tiled=True), projection...]
    all_gather x2 -> x0, blocking collectives: 6.27 us -> none  [the longest x1 4.42 us: per_device(): lax.all_gather(grad_rows, 'feat', axis=0, tiled=True)]
    unnamed x7 -> x9, local copies, waits for them, and re-layouts: 0.96 us -> 4.76 us
where the time goes in v1:
time: 29.3 us; the launch traced here: 29.1 us
  Pallas kernels  23.7 us (81%)
  local copies, waits for them, and re-layouts  4.76 us (16%)
  between operations  0.67 us (2%)
    pallas_call x1, Pallas kernels, per_device(): pl.pallas_call(functools.partial(kernel, sizes), out_shape=jax.ShapeDtype...  23.7 us
    unnamed x9, local copies, waits for them, and re-layouts  4.76 us

profile of v1, /device:TPU:0, one launch (start us, length us, event | category | flops | bytes accessed | tf_op | source)
XLA Modules:
  0.0 29.1 jit_solution(17025673335868902734)
XLA Ops:
  0.7 0.0 copy-start
  0.7 1.6 %copy-done = bf16[1,128,8192]{2,1,0:T(8,128)(2,1)S(1)} copy-done((bf16[1,128,8192]{2,1,0:T(8,128)(2,1)S(1)}, bf16[1,128,8192]{2,1,0:T(8,128)(2,1)}, u32[]{:S(2)}) %copy-start) | copy-done | bytes 2097176
  2.2 0.0 copy-start.1
  2.2 0.9 %copy-done.1 = bf16[1,128,1024]{2,1,0:T(8,128)(2,1)S(1)} copy-done((bf16[1,128,1024]{2,1,0:T(8,128)(2,1)S(1)}, bf16[1,128,1024]{2,1,0:T(8,128)(2,1)}, u32[]{:S(2)}) %copy-start.1) | copy-done | bytes 262168
  3.2 0.0 copy-start.2
  3.2 0.9 %copy-done.2 = bf16[8192,16]{0,1:T(8,128)(2,1)S(1)} copy-done((bf16[8192,16]{0,1:T(8,128)(2,1)S(1)}, bf16[8192,16]{0,1:T(8,128)(2,1)}, u32[]{:S(2)}) %copy-start.2) | copy-done | bytes 262168
  4.1 0.0 copy-start.3
  4.1 0.7 %copy-done.3 = s32[4]{0:T(128)S(1)} copy-done((s32[4]{0:T(128)S(1)}, s32[4]{0:T(128)}, u32[]{:S(2)}) %copy-start.3) | copy-done | bytes 40
  4.8 23.7 %shard_map.64 = f32[2,4096]{1,0:T(2,128)S(1)} custom-call(s32[1]{0:T(128)S(6)} %copy.8.lengths_ref, s32[4]{0:T(128)S(1)} %copy-done.3, bf16[1,128,8192]{2,1,0:T(8,128)(2,1)S(1)} %copy-done, bf16[1,128,1024]{2,1,0:T(8,128)(2,1)S(1)} %copy-done.1, bf16[16,8192]{1,0:T(8,128)(2,1)S(1)} %bitcast.1, bf16[4096,4096]{1,0:T(8,128)(2,1)} %projection_ref.1), custom_call_target="tpu_custom_call" | custom-call | tf_op jit(solution)/shard_map/pallas_call | solution.py:299
  28.5 0.6 %copy.9 = f32[2,4096]{1,0:T(2,128)} copy(f32[2,4096]{1,0:T(2,128)S(1)} %shard_map.64) | data formatting | bytes 65536
Async XLA Ops:
  0.7 1.6 %copy-start = (bf16[1,128,8192]{2,1,0:T(8,128)(2,1)S(1)}, bf16[1,128,8192]{2,1,0:T(8,128)(2,1)}, u32[]{:S(2)}) copy-start(bf16[1,128,8192]{2,1,0:T(8,128)(2,1)} %hidden_ref.1) | copy-start | bytes 6291460
  2.2 0.9 %copy-start.1 = (bf16[1,128,1024]{2,1,0:T(8,128)(2,1)S(1)}, bf16[1,128,1024]{2,1,0:T(8,128)(2,1)}, u32[]{:S(2)}) copy-start(bf16[1,128,1024]{2,1,0:T(8,128)(2,1)} %cotangent_ref.1) | copy-start | bytes 786436
  3.2 0.9 %copy-start.2 = (bf16[8192,16]{0,1:T(8,128)(2,1)S(1)}, bf16[8192,16]{0,1:T(8,128)(2,1)}, u32[]{:S(2)}) copy-start(bf16[8192,16]{0,1:T(8,128)(2,1)} %param.8) | copy-start | bytes 786436
  4.1 0.7 %copy-start.3 = (s32[4]{0:T(128)S(1)}, s32[4]{0:T(128)}, u32[]{:S(2)}) copy-start(s32[4]{0:T(128)} %order_ref.1) | copy-start | bytes 52

commit v2 on v1

v2 whole, which is shorter than its diff:
```python
import functools

import jax
import jax.numpy as jnp
from jax import lax
from jax.experimental import pallas as pl
from jax.experimental.pallas import tpu as pltpu
from jax.sharding import PartitionSpec as P

MESH = pl.DeviceIdType.MESH
F32 = jnp.float32
BF16 = jnp.bfloat16
FEATS = 8192
LANES = 128
HIDDEN_CHUNKS = 4


def loop(low, high, body):
    if high - low <= 4:
        for step in range(low, high):
            body(step)
    else:
        lax.fori_loop(low, high, lambda step, carry: (body(step), carry)[1], 0)


def kernel(
    sizes,
    lengths_ref, order_ref, hidden_ref, cotangent_ref, factor_ref, projection_ref,
    out_ref,
    lengths_v, order_v, hidden_v, cotangent_v, factor_v, projection_v,
    partial, partial_in, grads, grad_rows, rows_out, rows_in, final_out, final_in, squares_in,
    local_sem, projection_sem,
    grad_send, grad_recv, gather_send, gather_recv, rows_send, rows_recv,
    final_send, final_recv, squares_send, squares_recv,
):
    ctx_count, feat_count, ex_count = sizes
    ctx, feat, ex = lax.axis_index("ctx"), lax.axis_index("feat"), lax.axis_index("ex")
    slots = feat_count * ex_count
    slot = feat * ex_count + ex
    token_count, model_width = hidden_v.shape
    rank = factor_v.shape[0]
    own_rank = rank // ctx_count
    chunk_count, depth, chunk = projection_v.shape
    width = chunk_count * chunk
    value_width = cotangent_v.shape[1]
    padded = max(8, slots)
    own_ids = out_ref.shape[0]
    halves, half_rows = rows_out.shape[:2]

    step = model_width // HIDDEN_CHUNKS
    factor_copy = pltpu.make_async_copy(factor_ref, factor_v, local_sem.at[0])
    factor_copy.start()
    hidden_copies = []
    for k in range(HIDDEN_CHUNKS):
        columns = pl.ds(k * step, step)
        hidden_copies.append(
            pltpu.make_async_copy(
                hidden_ref.at[0, :, columns], hidden_v.at[:, columns], local_sem.at[4 + k]
            )
        )
        hidden_copies[-1].start()
    order_copy = pltpu.make_async_copy(order_ref, order_v, local_sem.at[2])
    order_copy.start()
    lengths_copy = pltpu.make_async_copy(lengths_ref, lengths_v, local_sem.at[3])
    lengths_copy.start()
    cotangent_copy = pltpu.make_async_copy(cotangent_ref.at[0], cotangent_v, local_sem.at[1])
    cotangent_copy.start()
    projection_copies = []
    for k in range(chunk_count):
        columns = pl.ds(pl.multiple_of(ex * width + k * chunk, LANES), chunk)
        projection_copies.append(
            pltpu.make_async_copy(
                projection_ref.at[:, columns], projection_v.at[k], projection_sem.at[k]
            )
        )
        projection_copies[-1].start()

    def ctx_peer(d):
        return lax.rem(ctx + d, ctx_count)

    def slot_peer(d):
        other = lax.rem(slot + d, slots)
        return other, {"feat": other // ex_count, "ex": lax.rem(other, ex_count)}

    barrier = pltpu.get_barrier_semaphore()

    def greet_ctx(d):
        pl.semaphore_signal(
            barrier, inc=1, device_id_type=MESH, device_id={"ctx": ctx_peer(d)}
        )

    def greet_slot(d):
        pl.semaphore_signal(
            barrier, inc=1, device_id_type=MESH, device_id=slot_peer(d)[1]
        )

    loop(1, ctx_count, greet_ctx)
    loop(1, slots, greet_slot)

    order_copy.wait()
    pick_shape = (own_rank * padded, slots * own_rank)
    row = lax.broadcasted_iota(jnp.int32, pick_shape, 0)
    column = lax.broadcasted_iota(jnp.int32, pick_shape, 1)
    column_id = jnp.zeros(pick_shape, jnp.int32)
    for s in range(slots):
        column_id = jnp.where(column // own_rank == s, order_v[s], column_id)
    pick = (row // padded == lax.rem(column, own_rank)) & (lax.rem(row, padded) == column_id)
    pick = pick.astype(F32).astype(BF16)

    lengths_copy.wait()
    factor_copy.wait()
    down = jnp.zeros((rank, token_count), F32)
    for k in range(HIDDEN_CHUNKS):
        hidden_copies[k].wait()
        columns = pl.ds(k * step, step)
        down += lax.dot_general(
            factor_v[:, columns], hidden_v[:, columns], (((1,), (1,)), ((), ())),
            preferred_element_type=F32,
        )
    position = ctx * token_count + lax.broadcasted_iota(jnp.int32, down.shape, 1)
    down = jnp.where(position < lengths_v[0], down, 0.0).astype(BF16)
    cotangent_copy.wait()
    grad = jnp.dot(down, cotangent_v[...], preferred_element_type=F32)
    for k in range(ctx_count):
        partial[k] = grad[k * own_rank:(k + 1) * own_rank]

    pl.semaphore_wait(barrier, ctx_count - 1 + slots - 1)

    def grad_copy(d, landing=None):
        other = ctx_peer(d)
        source = ctx if landing is None else other
        return pltpu.make_async_remote_copy(
            src_ref=partial.at[other], dst_ref=partial_in.at[source],
            send_sem=grad_send.at[d], recv_sem=grad_recv.at[source],
            device_id={"ctx": other}, device_id_type=MESH,
        )

    loop(1, ctx_count, lambda d: grad_copy(d).start())
    partial_in[ctx] = partial[ctx]
    loop(1, ctx_count, lambda d: grad_copy(d, True).wait_recv())
    total = partial_in[0]
    for k in range(1, ctx_count):
        total += partial_in[k]
    grads[slot] = total.astype(BF16).astype(F32)

    def gather_copy(d, landing=None):
        other, device = slot_peer(d)
        source = slot if landing is None else other
        return pltpu.make_async_remote_copy(
            src_ref=grads.at[source], dst_ref=grads.at[source],
            send_sem=gather_send.at[d], recv_sem=gather_recv.at[source],
            device_id=device, device_id_type=MESH,
        )

    loop(1, slots, lambda d: gather_copy(d).start())
    loop(1, slots, lambda d: gather_copy(d, True).wait_recv())
    for s in range(slots):
        grad_rows[s * own_rank:(s + 1) * own_rank] = grads[s]
    picked = jnp.dot(pick, grad_rows[...].astype(BF16), preferred_element_type=F32)
    left = [picked[r * padded:(r + 1) * padded].astype(BF16) for r in range(own_rank)]

    def rows_copy(h, d, landing=None):
        other = ctx_peer(d)
        source = ctx if landing is None else other
        return pltpu.make_async_remote_copy(
            src_ref=rows_out.at[h], dst_ref=rows_in.at[source, h],
            send_sem=rows_send.at[h, d], recv_sem=rows_recv.at[h, source],
            device_id={"ctx": other}, device_id_type=MESH,
        )

    per_half = chunk_count // halves
    for h in range(halves):
        for j in range(per_half):
            k = h * per_half + j
            projection_copies[k].wait()
            product = jnp.zeros((padded, chunk), F32)
            for r in range(own_rank):
                product += jnp.dot(
                    left[r], projection_v[k, r * value_width:(r + 1) * value_width, :],
                    preferred_element_type=F32,
                )
            rows_out[h, j * slots:(j + 1) * slots] = product[:slots]
        loop(1, ctx_count, lambda d: rows_copy(h, d).start())
        rows_in[ctx, h] = rows_out[h]

    for h in range(halves):
        loop(1, ctx_count, lambda d: rows_copy(h, d, True).wait_recv())
        summed = rows_in[0, h]
        for k in range(1, ctx_count):
            summed += rows_in[k, h]
        square = jnp.broadcast_to(
            jnp.sum(summed * summed, axis=1, keepdims=True), (half_rows, LANES)
        )
        for j in range(per_half):
            k = h * per_half + j
            for x in range(ex_count):
                here = slice(j * slots + x * own_ids, j * slots + (x + 1) * own_ids)
                there = slice(k * own_ids, (k + 1) * own_ids)
                final_out[x, there, :chunk] = summed[here]
                final_out[x, there, chunk:] = square[here]

    tail = pl.ds(chunk, LANES)

    def final_copy(d, landing=None):
        other = lax.rem(ex + d, ex_count)
        source = ex if landing is None else other
        return pltpu.make_async_remote_copy(
            src_ref=final_out.at[other], dst_ref=final_in.at[source],
            send_sem=final_send.at[d], recv_sem=final_recv.at[source],
            device_id={"ex": other}, device_id_type=MESH,
        )

    def squares_copy(q, landing=None):
        g, x = q // ex_count + 1, lax.rem(ex + lax.rem(q, ex_count), ex_count)
        other = lax.rem(feat + g, feat_count)
        source = slot if landing is None else other * ex_count + x
        return pltpu.make_async_remote_copy(
            src_ref=final_out.at[x, :, tail], dst_ref=squares_in.at[source],
            send_sem=squares_send.at[q], recv_sem=squares_recv.at[source],
            device_id={"feat": other, "ex": x}, device_id_type=MESH,
        )

    square_sends = (feat_count - 1) * ex_count
    loop(0, square_sends, lambda q: squares_copy(q).start())
    loop(1, ex_count, lambda d: final_copy(d).start())
    final_in[ex] = final_out[ex]
    loop(1, ex_count, lambda d: final_copy(d, True).wait_recv())
    for x in range(ex_count):
        squares_in[feat * ex_count + x] = final_in[x, :, chunk:]
    loop(0, square_sends, lambda q: squares_copy(q, True).wait_recv())
    everything = squares_in[0]
    for s in range(1, slots):
        everything += squares_in[s]
    norm = everything[:own_ids, :1]
    for k in range(1, chunk_count):
        norm += everything[k * own_ids:(k + 1) * own_ids, :1]
    norm = jnp.sqrt(norm / FEATS + 1e-06)
    for x in range(ex_count):
        for k in range(chunk_count):
            place = x * width + k * chunk
            out_ref[:, place:place + chunk] = final_in[x, k * own_ids:(k + 1) * own_ids, :chunk] / norm

    loop(1, ctx_count, lambda d: grad_copy(d).wait_send())
    loop(1, slots, lambda d: gather_copy(d).wait_send())
    for h in range(halves):
        loop(1, ctx_count, lambda d: rows_copy(h, d).wait_send())
    loop(1, ex_count, lambda d: final_copy(d).wait_send())
    loop(0, square_sends, lambda q: squares_copy(q).wait_send())


def per_device(sizes, hidden, cotangent, adapter_down_factor, projection, lengths, slot_example_order):
    ctx_count, feat_count, ex_count = sizes
    slots = feat_count * ex_count
    example_count, token_count, model_width = hidden.shape
    value_width = cotangent.shape[2]
    rank = adapter_down_factor.shape[1]
    depth, columns = projection.shape
    width = columns // ex_count
    chunk = min(512, width)
    chunk_count = width // chunk
    halves = 2 if chunk_count % 2 == 0 else 1
    own_ids = slots // ex_count
    own_rank = rank // ctx_count
    assert example_count == 1 and depth == own_rank * value_width
    dma = pltpu.SemaphoreType.DMA
    return pl.pallas_call(
        functools.partial(kernel, sizes),
        out_shape=jax.ShapeDtypeStruct((own_ids, columns), F32),
        in_specs=[pl.BlockSpec(memory_space=pltpu.HBM)] * 6,
        out_specs=pl.BlockSpec(memory_space=pltpu.VMEM),
        scratch_shapes=[
            pltpu.SMEM(lengths.shape, jnp.int32),
            pltpu.SMEM(slot_example_order.shape, jnp.int32),
            pltpu.VMEM((token_count, model_width), BF16),
            pltpu.VMEM((token_count, value_width), BF16),
            pltpu.VMEM((rank, model_width), BF16),
            pltpu.VMEM((chunk_count, depth, chunk), BF16),
            pltpu.VMEM((ctx_count, own_rank, value_width), F32),
            pltpu.VMEM((ctx_count, own_rank, value_width), F32),
            pltpu.VMEM((slots, own_rank, value_width), F32),
            pltpu.VMEM((slots * own_rank, value_width), F32),
            pltpu.VMEM((halves, chunk_count * slots // halves, chunk), F32),
            pltpu.VMEM((ctx_count, halves, chunk_count * slots // halves, chunk), F32),
            pltpu.VMEM((ex_count, chunk_count * own_ids, chunk + LANES), F32),
            pltpu.VMEM((ex_count, chunk_count * own_ids, chunk + LANES), F32),
            pltpu.VMEM((slots, chunk_count * own_ids, LANES), F32),
            dma((4 + HIDDEN_CHUNKS,)),
            dma((chunk_count,)),
            dma((ctx_count,)),
            dma((ctx_count,)),
            dma((slots,)),
            dma((slots,)),
            dma((halves, ctx_count)),
            dma((halves, ctx_count)),
            dma((ex_count,)),
            dma((ex_count,)),
            dma(((feat_count - 1) * ex_count,)),
            dma((slots,)),
        ],
        compiler_params=pltpu.CompilerParams(
            collective_id=0, has_side_effects=True, vmem_limit_bytes=60 * 1024 * 1024
        ),
    )(lengths, slot_example_order, hidden, cotangent, adapter_down_factor.T, projection)


def solution(mesh):
    in_specs = (
        P(("group", "feat", "ex"), "ctx", None),
        P(("group", "feat", "ex"), "ctx", None),
        P(),
        P("ctx", "feat"),
        P(("group", "feat", "ex")),
        P("group"),
    )
    out_specs = P(("group", "ex"), "feat")
    sizes = (mesh.shape["ctx"], mesh.shape["feat"], mesh.shape["ex"])
    return jax.shard_map(
        functools.partial(per_device, sizes),
        mesh=mesh, in_specs=in_specs, out_specs=out_specs, check_vma=False,
    )
```

time: 29.3 us -> 27.3 us (0.932)
  local copies, waits for them, and re-layouts: 4.76 us -> 1.38 us
  Pallas kernels: 23.7 us -> 25 us
    unnamed x9 -> x1, local copies, waits for them, and re-layouts: 4.76 us -> 1.38 us
    pallas_call x1, Pallas kernels: 23.7 us -> 25 us  [per_device(): pl.pallas_call(functools.partial(kernel, sizes), out_shape=jax.ShapeDtype...]
where the time goes in v2:
time: 27.3 us; the launch traced here: 27.1 us
  Pallas kernels  25 us (92%)
  local copies, waits for them, and re-layouts  1.38 us (5%)
  between operations  0.66 us (2%)
    pallas_call x1, Pallas kernels, per_device(): pl.pallas_call(functools.partial(kernel, sizes), out_shape=jax.ShapeDtype...  25 us
    unnamed x1, local copies, waits for them, and re-layouts  1.38 us

profile of v2, /device:TPU:0, one launch (start us, length us, event | category | flops | bytes accessed | tf_op | source)
XLA Modules:
  0.0 27.1 jit_solution(9410134199890021127)
XLA Ops:
  0.7 25.0 %shard_map.64 = f32[2,4096]{1,0:T(2,128)} custom-call(s32[1]{0:T(128)S(6)} %copy.8.lengths_ref, s32[4]{0:T(128)} %order_ref.1, bf16[1,128,8192]{2,1,0:T(8,128)(2,1)} %hidden_ref.1, bf16[1,128,1024]{2,1,0:T(8,128)(2,1)} %cotangent_ref.1, bf16[16,8192]{1,0:T(8,128)(2,1)} %bitcast.1, bf16[4096,4096]{1,0:T(8,128)(2,1)} %projection_ref.1), custom_call_target="tpu_custom_call" | custom-call | tf_op jit(solution)/shard_map/pallas_call | solution.py:266
  25.7 1.4 %copy.9 = f32[2,4096]{1,0:T(2,128)} copy(f32[2,4096]{1,0:T(2,128)} %shard_map.64) | data formatting | bytes 65536

commit v3 on v2

--- a/solution.py
+++ b/solution.py
@@ -10,13 +10,12 @@
 MESH = pl.DeviceIdType.MESH
 F32 = jnp.float32
 BF16 = jnp.bfloat16
-FEATS = 8192
 LANES = 128
 HIDDEN_CHUNKS = 4
 
 
 def loop(low, high, body):
-    if high - low <= 4:
+    if high - low <= 8:
         for step in range(low, high):
             body(step)
     else:
@@ -28,15 +27,19 @@
     lengths_ref, order_ref, hidden_ref, cotangent_ref, factor_ref, projection_ref,
     out_ref,
     lengths_v, order_v, hidden_v, cotangent_v, factor_v, projection_v,
-    partial, partial_in, grads, grad_rows, rows_out, rows_in, final_out, final_in, squares_in,
-    local_sem, projection_sem,
+    ids, partial, partial_in, grads, rows_out, rows_in, final_out, final_in, squares_in,
+    local_sem, projection_sem, ids_send, ids_recv,
     grad_send, grad_recv, gather_send, gather_recv, rows_send, rows_recv,
     final_send, final_recv, squares_send, squares_recv,
 ):
-    ctx_count, feat_count, ex_count = sizes
-    ctx, feat, ex = lax.axis_index("ctx"), lax.axis_index("feat"), lax.axis_index("ex")
-    slots = feat_count * ex_count
-    slot = feat * ex_count + ex
+    group_count, ctx_count, feat_count, ex_count = sizes
+    group, ctx, feat = lax.axis_index("group"), lax.axis_index("ctx"), lax.axis_index("feat")
+    ex = lax.axis_index("ex")
+    side_count = group_count * ex_count
+    side = group * ex_count + ex
+    slots = feat_count * side_count
+    slot = feat * side_count + side
+    group_slots = feat_count * ex_count
     token_count, model_width = hidden_v.shape
     rank = factor_v.shape[0]
     own_rank = rank // ctx_count
@@ -46,6 +49,8 @@
     padded = max(8, slots)
     own_ids = out_ref.shape[0]
     halves, half_rows = rows_out.shape[:2]
+    block, block_lanes = grads.shape[1:]
+    pieces = value_width // block_lanes
 
     step = model_width // HIDDEN_CHUNKS
     factor_copy = pltpu.make_async_copy(factor_ref, factor_v, local_sem.at[0])
@@ -67,20 +72,22 @@
     cotangent_copy.start()
     projection_copies = []
     for k in range(chunk_count):
-        columns = pl.ds(pl.multiple_of(ex * width + k * chunk, LANES), chunk)
+        columns = pl.ds(pl.multiple_of(side * width + k * chunk, LANES), chunk)
         projection_copies.append(
             pltpu.make_async_copy(
                 projection_ref.at[:, columns], projection_v.at[k], projection_sem.at[k]
             )
         )
-        projection_copies[-1].start()
+
+    def at_side(x):
+        return {"group": x // ex_count, "ex": lax.rem(x, ex_count)}
 
     def ctx_peer(d):
         return lax.rem(ctx + d, ctx_count)
 
     def slot_peer(d):
         other = lax.rem(slot + d, slots)
-        return other, {"feat": other // ex_count, "ex": lax.rem(other, ex_count)}
+        return other, {"feat": other // side_count, **at_side(lax.rem(other, side_count))}
 
     barrier = pltpu.get_barrier_semaphore()
 
@@ -98,20 +105,20 @@
     loop(1, slots, greet_slot)
 
     order_copy.wait()
-    pick_shape = (own_rank * padded, slots * own_rank)
-    row = lax.broadcasted_iota(jnp.int32, pick_shape, 0)
-    column = lax.broadcasted_iota(jnp.int32, pick_shape, 1)
-    column_id = jnp.zeros(pick_shape, jnp.int32)
-    for s in range(slots):
-        column_id = jnp.where(column // own_rank == s, order_v[s], column_id)
-    pick = (row // padded == lax.rem(column, own_rank)) & (lax.rem(row, padded) == column_id)
-    pick = pick.astype(F32).astype(BF16)
+    lane = lax.broadcasted_iota(jnp.int32, ids.shape[1:], 1)
+    own_order = jnp.zeros(ids.shape[1:], jnp.int32)
+    for i in range(group_slots):
+        own_order = jnp.where(lane == i, order_v[i], own_order)
+    ids[group] = own_order
 
     lengths_copy.wait()
     factor_copy.wait()
     down = jnp.zeros((rank, token_count), F32)
     for k in range(HIDDEN_CHUNKS):
         hidden_copies[k].wait()
+        if k == 1:
+            for copy in projection_copies:
+                copy.start()
         columns = pl.ds(k * step, step)
         down += lax.dot_general(
             factor_v[:, columns], hidden_v[:, columns], (((1,), (1,)), ((), ())),
@@ -135,13 +142,41 @@
             device_id={"ctx": other}, device_id_type=MESH,
         )
 
+    def ids_copy(d, landing=None):
+        other = lax.rem(group + d, group_count)
+        source = group if landing is None else other
+        return pltpu.make_async_remote_copy(
+            src_ref=ids.at[source], dst_ref=ids.at[source],
+            send_sem=ids_send.at[d], recv_sem=ids_recv.at[source],
+            device_id={"group": other}, device_id_type=MESH,
+        )
+
     loop(1, ctx_count, lambda d: grad_copy(d).start())
+    loop(1, group_count, lambda d: ids_copy(d).start())
     partial_in[ctx] = partial[ctx]
+
+    loop(1, group_count, lambda d: ids_copy(d, True).wait_recv())
+    pick_shape = (own_rank * pieces * padded, slots * block)
+    row = lax.broadcasted_iota(jnp.int32, pick_shape, 0)
+    column = lax.broadcasted_iota(jnp.int32, pick_shape, 1)
+    column_id = jnp.zeros(pick_shape, jnp.int32)
+    for f in range(feat_count):
+        for x in range(side_count):
+            i = f * ex_count + x % ex_count
+            value = ids[x // ex_count, :1, i:i + 1] + (x // ex_count) * group_slots
+            column_id = jnp.where(column // block == f * side_count + x, value, column_id)
+    wanted = lax.rem(row // padded, pieces) * own_rank + row // (padded * pieces)
+    pick = (lax.rem(column, block) == wanted) & (lax.rem(row, padded) == column_id)
+    pick = pick.astype(F32).astype(BF16)
+
     loop(1, ctx_count, lambda d: grad_copy(d, True).wait_recv())
     total = partial_in[0]
     for k in range(1, ctx_count):
         total += partial_in[k]
-    grads[slot] = total.astype(BF16).astype(F32)
+    rows = [total[:, q * block_lanes:(q + 1) * block_lanes] for q in range(pieces)]
+    if pieces * own_rank < block:
+        rows.append(jnp.zeros((block - pieces * own_rank, block_lanes), F32))
+    grads[slot] = jnp.concatenate(rows, axis=0).astype(BF16)
 
     def gather_copy(d, landing=None):
         other, device = slot_peer(d)
@@ -154,10 +189,9 @@
 
     loop(1, slots, lambda d: gather_copy(d).start())
     loop(1, slots, lambda d: gather_copy(d, True).wait_recv())
-    for s in range(slots):
-        grad_rows[s * own_rank:(s + 1) * own_rank] = grads[s]
-    picked = jnp.dot(pick, grad_rows[...].astype(BF16), preferred_element_type=F32)
-    left = [picked[r * padded:(r + 1) * padded].astype(BF16) for r in range(own_rank)]
+    gathered = grads[...].reshape(slots * block, block_lanes)
+    picked = jnp.dot(pick, gathered, preferred_element_type=F32)
+    left = [picked[i * padded:(i + 1) * padded].astype(BF16) for i in range(own_rank * pieces)]
 
     def rows_copy(h, d, landing=None):
         other = ctx_peer(d)
@@ -174,9 +208,9 @@
             k = h * per_half + j
             projection_copies[k].wait()
             product = jnp.zeros((padded, chunk), F32)
-            for r in range(own_rank):
+            for i in range(own_rank * pieces):
                 product += jnp.dot(
-                    left[r], projection_v[k, r * value_width:(r + 1) * value_width, :],
+                    left[i], projection_v[k, i * block_lanes:(i + 1) * block_lanes, :],
                     preferred_element_type=F32,
                 )
             rows_out[h, j * slots:(j + 1) * slots] = product[:slots]
@@ -193,7 +227,7 @@
         )
         for j in range(per_half):
             k = h * per_half + j
-            for x in range(ex_count):
+            for x in range(side_count):
                 here = slice(j * slots + x * own_ids, j * slots + (x + 1) * own_ids)
                 there = slice(k * own_ids, (k + 1) * own_ids)
                 final_out[x, there, :chunk] = summed[here]
@@ -202,31 +236,31 @@
     tail = pl.ds(chunk, LANES)
 
     def final_copy(d, landing=None):
-        other = lax.rem(ex + d, ex_count)
-        source = ex if landing is None else other
+        other = lax.rem(side + d, side_count)
+        source = side if landing is None else other
         return pltpu.make_async_remote_copy(
             src_ref=final_out.at[other], dst_ref=final_in.at[source],
             send_sem=final_send.at[d], recv_sem=final_recv.at[source],
-            device_id={"ex": other}, device_id_type=MESH,
+            device_id=at_side(other), device_id_type=MESH,
         )
 
     def squares_copy(q, landing=None):
-        g, x = q // ex_count + 1, lax.rem(ex + lax.rem(q, ex_count), ex_count)
+        g, x = q // side_count + 1, lax.rem(side + lax.rem(q, side_count), side_count)
         other = lax.rem(feat + g, feat_count)
-        source = slot if landing is None else other * ex_count + x
+        source = slot if landing is None else other * side_count + x
         return pltpu.make_async_remote_copy(
             src_ref=final_out.at[x, :, tail], dst_ref=squares_in.at[source],
             send_sem=squares_send.at[q], recv_sem=squares_recv.at[source],
-            device_id={"feat": other, "ex": x}, device_id_type=MESH,
-        )
-
-    square_sends = (feat_count - 1) * ex_count
+            device_id={"feat": other, **at_side(x)}, device_id_type=MESH,
+        )
+
+    square_sends = (feat_count - 1) * side_count
     loop(0, square_sends, lambda q: squares_copy(q).start())
-    loop(1, ex_count, lambda d: final_copy(d).start())
-    final_in[ex] = final_out[ex]
-    loop(1, ex_count, lambda d: final_copy(d, True).wait_recv())
-    for x in range(ex_count):
-        squares_in[feat * ex_count + x] = final_in[x, :, chunk:]
+    loop(1, side_count, lambda d: final_copy(d).start())
+    final_in[side] = final_out[side]
+    loop(1, side_count, lambda d: final_copy(d, True).wait_recv())
+    for x in range(side_count):
+        squares_in[feat * side_count + x] = final_in[x, :, chunk:]
     loop(0, square_sends, lambda q: squares_copy(q, True).wait_recv())
     everything = squares_in[0]
     for s in range(1, slots):
@@ -234,8 +268,8 @@
     norm = everything[:own_ids, :1]
     for k in range(1, chunk_count):
         norm += everything[k * own_ids:(k + 1) * own_ids, :1]
-    norm = jnp.sqrt(norm / FEATS + 1e-06)
-    for x in range(ex_count):
+    norm = jnp.sqrt(norm / (feat_count * side_count * width) + 1e-06)
+    for x in range(side_count):
         for k in range(chunk_count):
             place = x * width + k * chunk
             out_ref[:, place:place + chunk] = final_in[x, k * own_ids:(k + 1) * own_ids, :chunk] / norm
@@ -244,23 +278,27 @@
     loop(1, slots, lambda d: gather_copy(d).wait_send())
     for h in range(halves):
         loop(1, ctx_count, lambda d: rows_copy(h, d).wait_send())
-    loop(1, ex_count, lambda d: final_copy(d).wait_send())
+    loop(1, group_count, lambda d: ids_copy(d).wait_send())
+    loop(1, side_count, lambda d: final_copy(d).wait_send())
     loop(0, square_sends, lambda q: squares_copy(q).wait_send())
 
 
 def per_device(sizes, hidden, cotangent, adapter_down_factor, projection, lengths, slot_example_order):
-    ctx_count, feat_count, ex_count = sizes
-    slots = feat_count * ex_count
+    group_count, ctx_count, feat_count, ex_count = sizes
+    side_count = group_count * ex_count
+    slots = feat_count * side_count
     example_count, token_count, model_width = hidden.shape
     value_width = cotangent.shape[2]
     rank = adapter_down_factor.shape[1]
     depth, columns = projection.shape
-    width = columns // ex_count
+    width = columns // side_count
     chunk = min(512, width)
     chunk_count = width // chunk
     halves = 2 if chunk_count % 2 == 0 else 1
-    own_ids = slots // ex_count
+    own_ids = slots // side_count
     own_rank = rank // ctx_count
+    block_lanes = max(LANES, own_rank * value_width // 16)
+    block = -(-own_rank * value_width // block_lanes // 16) * 16
     assert example_count == 1 and depth == own_rank * value_width
     dma = pltpu.SemaphoreType.DMA
     return pl.pallas_call(
@@ -275,26 +313,28 @@
             pltpu.VMEM((token_count, value_width), BF16),
             pltpu.VMEM((rank, model_width), BF16),
             pltpu.VMEM((chunk_count, depth, chunk), BF16),
+            pltpu.VMEM((group_count, 8, LANES), jnp.int32),
             pltpu.VMEM((ctx_count, own_rank, value_width), F32),
             pltpu.VMEM((ctx_count, own_rank, value_width), F32),
-            pltpu.VMEM((slots, own_rank, value_width), F32),
-            pltpu.VMEM((slots * own_rank, value_width), F32),
+            pltpu.VMEM((slots, block, block_lanes), BF16),
             pltpu.VMEM((halves, chunk_count * slots // halves, chunk), F32),
             pltpu.VMEM((ctx_count, halves, chunk_count * slots // halves, chunk), F32),
-            pltpu.VMEM((ex_count, chunk_count * own_ids, chunk + LANES), F32),
-            pltpu.VMEM((ex_count, chunk_count * own_ids, chunk + LANES), F32),
+            pltpu.VMEM((side_count, chunk_count * own_ids, chunk + LANES), F32),
+            pltpu.VMEM((side_count, chunk_count * own_ids, chunk + LANES), F32),
             pltpu.VMEM((slots, chunk_count * own_ids, LANES), F32),
             dma((4 + HIDDEN_CHUNKS,)),
             dma((chunk_count,)),
+            dma((group_count,)),
+            dma((group_count,)),
             dma((ctx_count,)),
             dma((ctx_count,)),
             dma((slots,)),
             dma((slots,)),
             dma((halves, ctx_count)),
             dma((halves, ctx_count)),
-            dma((ex_count,)),
-            dma((ex_count,)),
-            dma(((feat_count - 1) * ex_count,)),
+            dma((side_count,)),
+            dma((side_count,)),
+            dma(((feat_count - 1) * side_count,)),
             dma((slots,)),
         ],
         compiler_params=pltpu.CompilerParams(
@@ -313,7 +353,7 @@
         P("group"),
     )
     out_specs = P(("group", "ex"), "feat")
-    sizes = (mesh.shape["ctx"], mesh.shape["feat"], mesh.shape["ex"])
+    sizes = (mesh.shape["group"], mesh.shape["ctx"], mesh.shape["feat"], mesh.shape["ex"])
     return jax.shard_map(
         functools.partial(per_device, sizes),
         mesh=mesh, in_specs=in_specs, out_specs=out_specs, check_vma=False,

time: 27.3 us -> 25.8 us (0.945)
  Pallas kernels: 25 us -> 23.6 us
    pallas_call x1, Pallas kernels: 25 us -> 23.6 us  [per_device(): pl.pallas_call(functools.partial(kernel, sizes), out_shape=jax.ShapeDtype...]
where the time goes in v3:
time: 25.8 us; the launch traced here: 25.6 us
  Pallas kernels  23.6 us (91%)
  local copies, waits for them, and re-layouts  1.38 us (5%)
  between operations  0.66 us (3%)
    pallas_call x1, Pallas kernels, per_device(): pl.pallas_call(functools.partial(kernel, sizes), out_shape=jax.ShapeDtype...  23.6 us
    unnamed x1, local copies, waits for them, and re-layouts  1.38 us

profile of v3, /device:TPU:0, one launch (start us, length us, event | category | flops | bytes accessed | tf_op | source)
XLA Modules:
  0.0 25.6 jit_solution(2122857337084910126)
XLA Ops:
  0.7 23.6 %shard_map.64 = f32[2,4096]{1,0:T(2,128)} custom-call(s32[1]{0:T(128)S(6)} %copy.8.lengths_ref, s32[4]{0:T(128)} %order_ref.1, bf16[1,128,8192]{2,1,0:T(8,128)(2,1)} %hidden_ref.1, bf16[1,128,1024]{2,1,0:T(8,128)(2,1)} %cotangent_ref.1, bf16[16,8192]{1,0:T(8,128)(2,1)} %bitcast.1, bf16[4096,4096]{1,0:T(8,128)(2,1)} %projection_ref.1), custom_call_target="tpu_custom_call" | custom-call | tf_op jit(solution)/shard_map/pallas_call | solution.py:304
  24.2 1.4 %copy.9 = f32[2,4096]{1,0:T(2,128)} copy(f32[2,4096]{1,0:T(2,128)} %shard_map.64) | data formatting | bytes 65536

commit v4 on v3

--- a/solution.py
+++ b/solution.py
@@ -48,35 +48,32 @@
     value_width = cotangent_v.shape[1]
     padded = max(8, slots)
     own_ids = out_ref.shape[0]
-    halves, half_rows = rows_out.shape[:2]
     block, block_lanes = grads.shape[1:]
     pieces = value_width // block_lanes
 
     step = model_width // HIDDEN_CHUNKS
     factor_copy = pltpu.make_async_copy(factor_ref, factor_v, local_sem.at[0])
     factor_copy.start()
-    hidden_copies = []
+
+    def hidden_copy(k):
+        columns = pl.ds(pl.multiple_of(k * step, LANES), step)
+        return pltpu.make_async_copy(
+            hidden_ref.at[0, :, columns], hidden_v.at[:, columns], local_sem.at[4 + k]
+        )
+
     for k in range(HIDDEN_CHUNKS):
-        columns = pl.ds(k * step, step)
-        hidden_copies.append(
-            pltpu.make_async_copy(
-                hidden_ref.at[0, :, columns], hidden_v.at[:, columns], local_sem.at[4 + k]
-            )
-        )
-        hidden_copies[-1].start()
+        hidden_copy(k).start()
     order_copy = pltpu.make_async_copy(order_ref, order_v, local_sem.at[2])
     order_copy.start()
     lengths_copy = pltpu.make_async_copy(lengths_ref, lengths_v, local_sem.at[3])
     lengths_copy.start()
     cotangent_copy = pltpu.make_async_copy(cotangent_ref.at[0], cotangent_v, local_sem.at[1])
     cotangent_copy.start()
-    projection_copies = []
-    for k in range(chunk_count):
+
+    def projection_copy(k):
         columns = pl.ds(pl.multiple_of(side * width + k * chunk, LANES), chunk)
-        projection_copies.append(
-            pltpu.make_async_copy(
-                projection_ref.at[:, columns], projection_v.at[k], projection_sem.at[k]
-            )
+        return pltpu.make_async_copy(
+            projection_ref.at[:, columns], projection_v.at[k], projection_sem.at[k]
         )
 
     def at_side(x):
@@ -113,17 +110,22 @@
 
     lengths_copy.wait()
     factor_copy.wait()
-    down = jnp.zeros((rank, token_count), F32)
-    for k in range(HIDDEN_CHUNKS):
-        hidden_copies[k].wait()
-        if k == 1:
-            for copy in projection_copies:
-                copy.start()
-        columns = pl.ds(k * step, step)
-        down += lax.dot_general(
+    hidden_copy(0).wait()
+    for k in range(chunk_count):
+        projection_copy(k).start()
+
+    def add_down(k, down):
+        @pl.when(k > 0)
+        def _():
+            hidden_copy(k).wait()
+
+        columns = pl.ds(pl.multiple_of(k * step, LANES), step)
+        return down + lax.dot_general(
             factor_v[:, columns], hidden_v[:, columns], (((1,), (1,)), ((), ())),
             preferred_element_type=F32,
         )
+
+    down = lax.fori_loop(0, HIDDEN_CHUNKS, add_down, jnp.zeros((rank, token_count), F32))
     position = ctx * token_count + lax.broadcasted_iota(jnp.int32, down.shape, 1)
     down = jnp.where(position < lengths_v[0], down, 0.0).astype(BF16)
     cotangent_copy.wait()
@@ -202,36 +204,35 @@
             device_id={"ctx": other}, device_id_type=MESH,
         )
 
-    per_half = chunk_count // halves
-    for h in range(halves):
-        for j in range(per_half):
-            k = h * per_half + j
-            projection_copies[k].wait()
-            product = jnp.zeros((padded, chunk), F32)
-            for i in range(own_rank * pieces):
-                product += jnp.dot(
-                    left[i], projection_v[k, i * block_lanes:(i + 1) * block_lanes, :],
-                    preferred_element_type=F32,
-                )
-            rows_out[h, j * slots:(j + 1) * slots] = product[:slots]
-        loop(1, ctx_count, lambda d: rows_copy(h, d).start())
-        rows_in[ctx, h] = rows_out[h]
-
-    for h in range(halves):
-        loop(1, ctx_count, lambda d: rows_copy(h, d, True).wait_recv())
-        summed = rows_in[0, h]
-        for k in range(1, ctx_count):
-            summed += rows_in[k, h]
+    def project(k, carry):
+        projection_copy(k).wait()
+        product = jnp.zeros((padded, chunk), F32)
+        for i in range(own_rank * pieces):
+            product += jnp.dot(
+                left[i], projection_v[k, i * block_lanes:(i + 1) * block_lanes, :],
+                preferred_element_type=F32,
+            )
+        rows_out[k] = product[:slots]
+        for d in range(1, ctx_count):
+            rows_copy(k, d).start()
+        rows_in[ctx, k] = product[:slots]
+        return carry
+
+    lax.fori_loop(0, chunk_count, project, 0)
+
+    for k in range(chunk_count):
+        loop(1, ctx_count, lambda d: rows_copy(k, d, True).wait_recv())
+        summed = rows_in[0, k]
+        for c in range(1, ctx_count):
+            summed += rows_in[c, k]
         square = jnp.broadcast_to(
-            jnp.sum(summed * summed, axis=1, keepdims=True), (half_rows, LANES)
-        )
-        for j in range(per_half):
-            k = h * per_half + j
-            for x in range(side_count):
-                here = slice(j * slots + x * own_ids, j * slots + (x + 1) * own_ids)
-                there = slice(k * own_ids, (k + 1) * own_ids)
-                final_out[x, there, :chunk] = summed[here]
-                final_out[x, there, chunk:] = square[here]
+            jnp.sum(summed * summed, axis=1, keepdims=True), (slots, LANES)
+        )
+        there = slice(k * own_ids, (k + 1) * own_ids)
+        for x in range(side_count):
+            here = slice(x * own_ids, (x + 1) * own_ids)
+            final_out[x, there, :chunk] = summed[here]
+            final_out[x, there, chunk:] = square[here]
 
     tail = pl.ds(chunk, LANES)
 
@@ -276,8 +277,8 @@
 
     loop(1, ctx_count, lambda d: grad_copy(d).wait_send())
     loop(1, slots, lambda d: gather_copy(d).wait_send())
-    for h in range(halves):
-        loop(1, ctx_count, lambda d: rows_copy(h, d).wait_send())
+    for k in range(chunk_count):
+        loop(1, ctx_count, lambda d: rows_copy(k, d).wait_send())
     loop(1, group_count, lambda d: ids_copy(d).wait_send())
     loop(1, side_count, lambda d: final_copy(d).wait_send())
     loop(0, square_sends, lambda q: squares_copy(q).wait_send())
@@ -292,9 +293,8 @@
     rank = adapter_down_factor.shape[1]
     depth, columns = projection.shape
     width = columns // side_count
-    chunk = min(512, width)
+    chunk = min(256, width)
     chunk_count = width // chunk
-    halves = 2 if chunk_count % 2 == 0 else 1
     own_ids = slots // side_count
     own_rank = rank // ctx_count
     block_lanes = max(LANES, own_rank * value_width // 16)
@@ -317,8 +317,8 @@
             pltpu.VMEM((ctx_count, own_rank, value_width), F32),
             pltpu.VMEM((ctx_count, own_rank, value_width), F32),
             pltpu.VMEM((slots, block, block_lanes), BF16),
-            pltpu.VMEM((halves, chunk_count * slots // halves, chunk), F32),
-            pltpu.VMEM((ctx_count, halves, chunk_count * slots // halves, chunk), F32),
+            pltpu.VMEM((chunk_count, slots, chunk), F32),
+            pltpu.VMEM((ctx_count, chunk_count, slots, chunk), F32),
             pltpu.VMEM((side_count, chunk_count * own_ids, chunk + LANES), F32),
             pltpu.VMEM((side_count, chunk_count * own_ids, chunk + LANES), F32),
             pltpu.VMEM((slots, chunk_count * own_ids, LANES), F32),
@@ -330,8 +330,8 @@
             dma((ctx_count,)),
             dma((slots,)),
             dma((slots,)),
-            dma((halves, ctx_count)),
-            dma((halves, ctx_count)),
+            dma((chunk_count, ctx_count)),
+            dma((chunk_count, ctx_count)),
             dma((side_count,)),
             dma((side_count,)),
             dma(((feat_count - 1) * side_count,)),

time: 25.8 us -> 25.1 us (0.973)
  Pallas kernels: 23.6 us -> 22.9 us
    pallas_call x1, Pallas kernels: 23.6 us -> 22.9 us  [per_device(): pl.pallas_call(functools.partial(kernel, sizes), out_shape=jax.ShapeDtype...]
where the time goes in v4:
time: 25.1 us; the launch traced here: 24.9 us
  Pallas kernels  22.9 us (91%)
  local copies, waits for them, and re-layouts  1.38 us (5%)
  between operations  0.66 us (3%)
    pallas_call x1, Pallas kernels, per_device(): pl.pallas_call(functools.partial(kernel, sizes), out_shape=jax.ShapeDtype...  22.9 us
    unnamed x1, local copies, waits for them, and re-layouts  1.38 us

profile of v4, /device:TPU:0, one launch (start us, length us, event | category | flops | bytes accessed | tf_op | source)
XLA Modules:
  0.0 24.9 jit_solution(15421531618564935616)
XLA Ops:
  0.7 22.9 %shard_map.64 = f32[2,4096]{1,0:T(2,128)} custom-call(s32[1]{0:T(128)S(6)} %copy.8.lengths_ref, s32[4]{0:T(128)} %order_ref.1, bf16[1,128,8192]{2,1,0:T(8,128)(2,1)} %hidden_ref.1, bf16[1,128,1024]{2,1,0:T(8,128)(2,1)} %cotangent_ref.1, bf16[16,8192]{1,0:T(8,128)(2,1)} %bitcast.1, bf16[4096,4096]{1,0:T(8,128)(2,1)} %projection_ref.1), custom_call_target="tpu_custom_call" | custom-call | tf_op jit(solution)/shard_map/pallas_call | solution.py:304
  23.6 1.4 %copy.9 = f32[2,4096]{1,0:T(2,128)} copy(f32[2,4096]{1,0:T(2,128)} %shard_map.64) | data formatting | bytes 65536

commit v5 on v4

--- a/solution.py
+++ b/solution.py
@@ -212,27 +212,30 @@
                 left[i], projection_v[k, i * block_lanes:(i + 1) * block_lanes, :],
                 preferred_element_type=F32,
             )
-        rows_out[k] = product[:slots]
+        lanes = [product[:slots, p * LANES:(p + 1) * LANES] for p in range(chunk // LANES)]
+        rows_out[k] = jnp.concatenate(lanes, axis=0).astype(BF16)
         for d in range(1, ctx_count):
             rows_copy(k, d).start()
-        rows_in[ctx, k] = product[:slots]
+        rows_in[ctx, k] = rows_out[k]
         return carry
 
     lax.fori_loop(0, chunk_count, project, 0)
 
     for k in range(chunk_count):
         loop(1, ctx_count, lambda d: rows_copy(k, d, True).wait_recv())
-        summed = rows_in[0, k]
+        summed = rows_in[0, k].astype(F32)
         for c in range(1, ctx_count):
-            summed += rows_in[c, k]
-        square = jnp.broadcast_to(
-            jnp.sum(summed * summed, axis=1, keepdims=True), (slots, LANES)
-        )
+            summed += rows_in[c, k].astype(F32)
+        lanes = [summed[p * slots:(p + 1) * slots] for p in range(chunk // LANES)]
+        square = lanes[0] * lanes[0]
+        for part in lanes[1:]:
+            square += part * part
+        square = jnp.broadcast_to(jnp.sum(square, axis=1, keepdims=True), (slots, LANES))
         there = slice(k * own_ids, (k + 1) * own_ids)
         for x in range(side_count):
             here = slice(x * own_ids, (x + 1) * own_ids)
-            final_out[x, there, :chunk] = summed[here]
-            final_out[x, there, chunk:] = square[here]
+            for p, part in enumerate(lanes + [square]):
+                final_out[x, there, p * LANES:(p + 1) * LANES] = part[here]
 
     tail = pl.ds(chunk, LANES)
 
@@ -317,8 +320,8 @@
             pltpu.VMEM((ctx_count, own_rank, value_width), F32),
             pltpu.VMEM((ctx_count, own_rank, value_width), F32),
             pltpu.VMEM((slots, block, block_lanes), BF16),
-            pltpu.VMEM((chunk_count, slots, chunk), F32),
-            pltpu.VMEM((ctx_count, chunk_count, slots, chunk), F32),
+            pltpu.VMEM((chunk_count, slots * chunk // LANES, LANES), BF16),
+            pltpu.VMEM((ctx_count, chunk_count, slots * chunk // LANES, LANES), BF16),
             pltpu.VMEM((side_count, chunk_count * own_ids, chunk + LANES), F32),
             pltpu.VMEM((side_count, chunk_count * own_ids, chunk + LANES), F32),
             pltpu.VMEM((slots, chunk_count * own_ids, LANES), F32),
@@ -338,7 +341,7 @@
             dma((slots,)),
         ],
         compiler_params=pltpu.CompilerParams(
-            collective_id=0, has_side_effects=True, vmem_limit_bytes=60 * 1024 * 1024
+            collective_id=0, has_side_effects=True, vmem_limit_bytes=215 * 1024 * 256
         ),
     )(lengths, slot_example_order, hidden, cotangent, adapter_down_factor.T, projection)
 

time: 25.1 us -> 24 us (0.956)
  Pallas kernels: 22.9 us -> 21.9 us
    pallas_call x1, Pallas kernels: 22.9 us -> 21.9 us  [per_device(): pl.pallas_call(functools.partial(kernel, sizes), out_shape=jax.ShapeDtype...]
    unnamed x1 -> x3, local copies, waits for them, and re-layouts: 1.38 us -> 1.27 us
where the time goes in v5:
time: 24 us; the launch traced here: 23.8 us
  Pallas kernels  21.9 us (91%)
  local copies, waits for them, and re-layouts  1.27 us (5%)
  between operations  0.67 us (3%)
    pallas_call x1, Pallas kernels, per_device(): pl.pallas_call(functools.partial(kernel, sizes), out_shape=jax.ShapeDtype...  21.9 us
    unnamed x3, local copies, waits for them, and re-layouts  1.27 us

profile of v5, /device:TPU:0, one launch (start us, length us, event | category | flops | bytes accessed | tf_op | source)
XLA Modules:
  0.0 23.8 jit_solution(15957552204774142423)
XLA Ops:
  0.7 0.0 copy-start
  0.7 0.6 %copy-done = s32[4]{0:T(128)S(1)} copy-done((s32[4]{0:T(128)S(1)}, s32[4]{0:T(128)}, u32[]{:S(2)}) %copy-start) | copy-done | bytes 40
  1.3 21.9 %shard_map.64 = f32[2,4096]{1,0:T(2,128)S(1)} custom-call(s32[1]{0:T(128)S(6)} %copy.8.lengths_ref, s32[4]{0:T(128)S(1)} %copy-done, bf16[1,128,8192]{2,1,0:T(8,128)(2,1)} %hidden_ref.1, bf16[1,128,1024]{2,1,0:T(8,128)(2,1)} %cotangent_ref.1, bf16[16,8192]{1,0:T(8,128)(2,1)} %bitcast.1, bf16[4096,4096]{1,0:T(8,128)(2,1)} %projection_ref.1), custom_call_target="tpu_custom_call" | custom-call | tf_op jit(solution)/shard_map/pallas_call | solution.py:307
  23.2 0.6 %copy.9 = f32[2,4096]{1,0:T(2,128)} copy(f32[2,4096]{1,0:T(2,128)S(1)} %shard_map.64) | data formatting | bytes 65536
Async XLA Ops:
  0.7 0.7 %copy-start = (s32[4]{0:T(128)S(1)}, s32[4]{0:T(128)}, u32[]{:S(2)}) copy-start(s32[4]{0:T(128)} %order_ref.1) | copy-start | bytes 52

commit v6 on v4

--- a/solution.py
+++ b/solution.py
@@ -15,7 +15,7 @@
 
 
 def loop(low, high, body):
-    if high - low <= 8:
+    if high - low <= 16:
         for step in range(low, high):
             body(step)
     else:
@@ -27,10 +27,10 @@
     lengths_ref, order_ref, hidden_ref, cotangent_ref, factor_ref, projection_ref,
     out_ref,
     lengths_v, order_v, hidden_v, cotangent_v, factor_v, projection_v,
-    ids, partial, partial_in, grads, rows_out, rows_in, final_out, final_in, squares_in,
+    ids, partial, partial_in, grads, products, rows_out, rows_in, squares,
     local_sem, projection_sem, ids_send, ids_recv,
     grad_send, grad_recv, gather_send, gather_recv, rows_send, rows_recv,
-    final_send, final_recv, squares_send, squares_recv,
+    squares_send, squares_recv,
 ):
     group_count, ctx_count, feat_count, ex_count = sizes
     group, ctx, feat = lax.axis_index("group"), lax.axis_index("ctx"), lax.axis_index("feat")
@@ -86,20 +86,29 @@
         other = lax.rem(slot + d, slots)
         return other, {"feat": other // side_count, **at_side(lax.rem(other, side_count))}
 
+    def owner_peer(q):
+        c = lax.rem(ctx + q // side_count, ctx_count)
+        x = lax.rem(side + lax.rem(q, side_count), side_count)
+        return c, x, {"ctx": c, **at_side(x)}
+
     barrier = pltpu.get_barrier_semaphore()
 
-    def greet_ctx(d):
+    def greet_owner(q):
         pl.semaphore_signal(
-            barrier, inc=1, device_id_type=MESH, device_id={"ctx": ctx_peer(d)}
-        )
-
-    def greet_slot(d):
+            barrier, inc=1, device_id_type=MESH, device_id=owner_peer(q)[2]
+        )
+
+    def greet_feat(q):
+        other = lax.rem(feat + 1 + q // side_count, feat_count)
         pl.semaphore_signal(
-            barrier, inc=1, device_id_type=MESH, device_id=slot_peer(d)[1]
-        )
-
-    loop(1, ctx_count, greet_ctx)
-    loop(1, slots, greet_slot)
+            barrier, inc=1, device_id_type=MESH,
+            device_id={"feat": other, **at_side(lax.rem(q, side_count))},
+        )
+
+    owners = ctx_count * side_count
+    others = (feat_count - 1) * side_count
+    loop(1, owners, greet_owner)
+    loop(0, others, greet_feat)
 
     order_copy.wait()
     lane = lax.broadcasted_iota(jnp.int32, ids.shape[1:], 1)
@@ -133,7 +142,7 @@
     for k in range(ctx_count):
         partial[k] = grad[k * own_rank:(k + 1) * own_rank]
 
-    pl.semaphore_wait(barrier, ctx_count - 1 + slots - 1)
+    pl.semaphore_wait(barrier, owners - 1 + others)
 
     def grad_copy(d, landing=None):
         other = ctx_peer(d)
@@ -195,15 +204,6 @@
     picked = jnp.dot(pick, gathered, preferred_element_type=F32)
     left = [picked[i * padded:(i + 1) * padded].astype(BF16) for i in range(own_rank * pieces)]
 
-    def rows_copy(h, d, landing=None):
-        other = ctx_peer(d)
-        source = ctx if landing is None else other
-        return pltpu.make_async_remote_copy(
-            src_ref=rows_out.at[h], dst_ref=rows_in.at[source, h],
-            send_sem=rows_send.at[h, d], recv_sem=rows_recv.at[h, source],
-            device_id={"ctx": other}, device_id_type=MESH,
-        )
-
     def project(k, carry):
         projection_copy(k).wait()
         product = jnp.zeros((padded, chunk), F32)
@@ -212,76 +212,72 @@
                 left[i], projection_v[k, i * block_lanes:(i + 1) * block_lanes, :],
                 preferred_element_type=F32,
             )
-        rows_out[k] = product[:slots]
-        for d in range(1, ctx_count):
-            rows_copy(k, d).start()
-        rows_in[ctx, k] = product[:slots]
+        products[k] = product[:slots]
         return carry
 
     lax.fori_loop(0, chunk_count, project, 0)
 
-    for k in range(chunk_count):
-        loop(1, ctx_count, lambda d: rows_copy(k, d, True).wait_recv())
-        summed = rows_in[0, k]
+    def rows_copy(q, landing=None):
+        c, x, device = owner_peer(q)
+        source = (ctx, side) if landing is None else (c, x)
+        return pltpu.make_async_remote_copy(
+            src_ref=rows_out.at[x], dst_ref=rows_in.at[source[0], source[1]],
+            send_sem=rows_send.at[q], recv_sem=rows_recv.at[source[0], source[1]],
+            device_id=device, device_id_type=MESH,
+        )
+
+    tiles = chunk // LANES
+    for x in range(side_count):
+        rows_out[x] = jnp.concatenate(
+            [
+                products[k, x * own_ids:(x + 1) * own_ids, p * LANES:(p + 1) * LANES]
+                for k in range(chunk_count) for p in range(tiles)
+            ],
+            axis=0,
+        ).astype(BF16)
+    loop(1, owners, lambda q: rows_copy(q).start())
+    rows_in[ctx, side] = rows_out[side]
+    loop(1, owners, lambda q: rows_copy(q, True).wait_recv())
+    summed = []
+    for x in range(side_count):
+        summed.append(rows_in[0, x].astype(F32))
         for c in range(1, ctx_count):
-            summed += rows_in[c, k]
-        square = jnp.broadcast_to(
-            jnp.sum(summed * summed, axis=1, keepdims=True), (slots, LANES)
-        )
-        there = slice(k * own_ids, (k + 1) * own_ids)
-        for x in range(side_count):
-            here = slice(x * own_ids, (x + 1) * own_ids)
-            final_out[x, there, :chunk] = summed[here]
-            final_out[x, there, chunk:] = square[here]
-
-    tail = pl.ds(chunk, LANES)
-
-    def final_copy(d, landing=None):
-        other = lax.rem(side + d, side_count)
-        source = side if landing is None else other
-        return pltpu.make_async_remote_copy(
-            src_ref=final_out.at[other], dst_ref=final_in.at[source],
-            send_sem=final_send.at[d], recv_sem=final_recv.at[source],
-            device_id=at_side(other), device_id_type=MESH,
-        )
-
-    def squares_copy(q, landing=None):
-        g, x = q // side_count + 1, lax.rem(side + lax.rem(q, side_count), side_count)
-        other = lax.rem(feat + g, feat_count)
-        source = slot if landing is None else other * side_count + x
-        return pltpu.make_async_remote_copy(
-            src_ref=final_out.at[x, :, tail], dst_ref=squares_in.at[source],
-            send_sem=squares_send.at[q], recv_sem=squares_recv.at[source],
-            device_id={"feat": other, **at_side(x)}, device_id_type=MESH,
-        )
-
-    square_sends = (feat_count - 1) * side_count
-    loop(0, square_sends, lambda q: squares_copy(q).start())
-    loop(1, side_count, lambda d: final_copy(d).start())
-    final_in[side] = final_out[side]
-    loop(1, side_count, lambda d: final_copy(d, True).wait_recv())
+            summed[x] += rows_in[c, x].astype(F32)
+
+    square = summed[0] * summed[0]
+    for part in summed[1:]:
+        square += part * part
+    square = jnp.sum(square, axis=1, keepdims=True)
+    own_square = square[:own_ids]
+    for t in range(1, chunk_count * tiles):
+        own_square += square[t * own_ids:(t + 1) * own_ids]
+    squares[feat] = jnp.broadcast_to(own_square, (own_ids, LANES))
+
+    def squares_copy(d, landing=None):
+        other = lax.rem(feat + d, feat_count)
+        source = feat if landing is None else other
+        return pltpu.make_async_remote_copy(
+            src_ref=squares.at[source], dst_ref=squares.at[source],
+            send_sem=squares_send.at[d], recv_sem=squares_recv.at[source],
+            device_id={"feat": other}, device_id_type=MESH,
+        )
+
+    loop(1, feat_count, lambda d: squares_copy(d).start())
+    loop(1, feat_count, lambda d: squares_copy(d, True).wait_recv())
+    everything = squares[0]
+    for f in range(1, feat_count):
+        everything += squares[f]
+    norm = jnp.sqrt(everything / (feat_count * side_count * width) + 1e-06)
     for x in range(side_count):
-        squares_in[feat * side_count + x] = final_in[x, :, chunk:]
-    loop(0, square_sends, lambda q: squares_copy(q, True).wait_recv())
-    everything = squares_in[0]
-    for s in range(1, slots):
-        everything += squares_in[s]
-    norm = everything[:own_ids, :1]
-    for k in range(1, chunk_count):
-        norm += everything[k * own_ids:(k + 1) * own_ids, :1]
-    norm = jnp.sqrt(norm / (feat_count * side_count * width) + 1e-06)
-    for x in range(side_count):
-        for k in range(chunk_count):
-            place = x * width + k * chunk
-            out_ref[:, place:place + chunk] = final_in[x, k * own_ids:(k + 1) * own_ids, :chunk] / norm
+        for t in range(chunk_count * tiles):
+            place = x * width + t * LANES
+            out_ref[:, place:place + LANES] = summed[x][t * own_ids:(t + 1) * own_ids] / norm
 
     loop(1, ctx_count, lambda d: grad_copy(d).wait_send())
     loop(1, slots, lambda d: gather_copy(d).wait_send())
-    for k in range(chunk_count):
-        loop(1, ctx_count, lambda d: rows_copy(k, d).wait_send())
+    loop(1, owners, lambda q: rows_copy(q).wait_send())
     loop(1, group_count, lambda d: ids_copy(d).wait_send())
-    loop(1, side_count, lambda d: final_copy(d).wait_send())
-    loop(0, square_sends, lambda q: squares_copy(q).wait_send())
+    loop(1, feat_count, lambda d: squares_copy(d).wait_send())
 
 
 def per_device(sizes, hidden, cotangent, adapter_down_factor, projection, lengths, slot_example_order):
@@ -318,10 +314,9 @@
             pltpu.VMEM((ctx_count, own_rank, value_width), F32),
             pltpu.VMEM((slots, block, block_lanes), BF16),
             pltpu.VMEM((chunk_count, slots, chunk), F32),
-            pltpu.VMEM((ctx_count, chunk_count, slots, chunk), F32),
-            pltpu.VMEM((side_count, chunk_count * own_ids, chunk + LANES), F32),
-            pltpu.VMEM((side_count, chunk_count * own_ids, chunk + LANES), F32),
-            pltpu.VMEM((slots, chunk_count * own_ids, LANES), F32),
+            pltpu.VMEM((side_count, width // LANES * own_ids, LANES), BF16),
+            pltpu.VMEM((ctx_count, side_count, width // LANES * own_ids, LANES), BF16),
+            pltpu.VMEM((feat_count, own_ids, LANES), F32),
             dma((4 + HIDDEN_CHUNKS,)),
             dma((chunk_count,)),
             dma((group_count,)),
@@ -330,15 +325,13 @@
             dma((ctx_count,)),
             dma((slots,)),
             dma((slots,)),
-            dma((chunk_count, ctx_count)),
-            dma((chunk_count, ctx_count)),
-            dma((side_count,)),
-            dma((side_count,)),
-            dma(((feat_count - 1) * side_count,)),
-            dma((slots,)),
+            dma((ctx_count * side_count,)),
+            dma((ctx_count, side_count)),
+            dma((feat_count,)),
+            dma((feat_count,)),
         ],
         compiler_params=pltpu.CompilerParams(
-            collective_id=0, has_side_effects=True, vmem_limit_bytes=60 * 1024 * 1024
+            collective_id=0, has_side_effects=True, vmem_limit_bytes=215 * 1024 * 256
         ),
     )(lengths, slot_example_order, hidden, cotangent, adapter_down_factor.T, projection)
 

time: 25.1 us -> 24.7 us (0.984)
  Pallas kernels: 22.9 us -> 22.6 us
    pallas_call x1, Pallas kernels: 22.9 us -> 22.6 us  [per_device(): pl.pallas_call(functools.partial(kernel, sizes), out_shape=jax.ShapeDtype...]
    unnamed x1 -> x3, local copies, waits for them, and re-layouts: 1.38 us -> 1.27 us
where the time goes in v6:
time: 24.7 us; the launch traced here: 24.5 us
  Pallas kernels  22.6 us (91%)
  local copies, waits for them, and re-layouts  1.27 us (5%)
  between operations  0.67 us (3%)
    pallas_call x1, Pallas kernels, per_device(): pl.pallas_call(functools.partial(kernel, sizes), out_shape=jax.ShapeDtype...  22.6 us
    unnamed x3, local copies, waits for them, and re-layouts  1.27 us

profile of v6, /device:TPU:0, one launch (start us, length us, event | category | flops | bytes accessed | tf_op | source)
XLA Modules:
  0.0 24.5 jit_solution(4986247039651045784)
XLA Ops:
  0.7 0.0 copy-start
  0.7 0.6 %copy-done = s32[4]{0:T(128)S(1)} copy-done((s32[4]{0:T(128)S(1)}, s32[4]{0:T(128)}, u32[]{:S(2)}) %copy-start) | copy-done | bytes 40
  1.3 22.6 %shard_map.64 = f32[2,4096]{1,0:T(2,128)S(1)} custom-call(s32[1]{0:T(128)S(6)} %copy.8.lengths_ref, s32[4]{0:T(128)S(1)} %copy-done, bf16[1,128,8192]{2,1,0:T(8,128)(2,1)} %hidden_ref.1, bf16[1,128,1024]{2,1,0:T(8,128)(2,1)} %cotangent_ref.1, bf16[16,8192]{1,0:T(8,128)(2,1)} %bitcast.1, bf16[4096,4096]{1,0:T(8,128)(2,1)} %projection_ref.1), custom_call_target="tpu_custom_call" | custom-call | tf_op jit(solution)/shard_map/pallas_call | solution.py:300
  23.9 0.6 %copy.9 = f32[2,4096]{1,0:T(2,128)} copy(f32[2,4096]{1,0:T(2,128)S(1)} %shard_map.64) | data formatting | bytes 65536
Async XLA Ops:
  0.7 0.7 %copy-start = (s32[4]{0:T(128)S(1)}, s32[4]{0:T(128)}, u32[]{:S(2)}) copy-start(s32[4]{0:T(128)} %order_ref.1) | copy-start | bytes 52

commit v7 on v5

--- a/solution.py
+++ b/solution.py
@@ -121,15 +121,17 @@
 
         columns = pl.ds(pl.multiple_of(k * step, LANES), step)
         return down + lax.dot_general(
-            factor_v[:, columns], hidden_v[:, columns], (((1,), (1,)), ((), ())),
+            hidden_v[:, columns], factor_v[:, columns], (((1,), (1,)), ((), ())),
             preferred_element_type=F32,
         )
 
-    down = lax.fori_loop(0, HIDDEN_CHUNKS, add_down, jnp.zeros((rank, token_count), F32))
-    position = ctx * token_count + lax.broadcasted_iota(jnp.int32, down.shape, 1)
+    down = lax.fori_loop(0, HIDDEN_CHUNKS, add_down, jnp.zeros((token_count, rank), F32))
+    position = ctx * token_count + lax.broadcasted_iota(jnp.int32, down.shape, 0)
     down = jnp.where(position < lengths_v[0], down, 0.0).astype(BF16)
     cotangent_copy.wait()
-    grad = jnp.dot(down, cotangent_v[...], preferred_element_type=F32)
+    grad = lax.dot_general(
+        down, cotangent_v[...], (((0,), (0,)), ((), ())), preferred_element_type=F32
+    )
     for k in range(ctx_count):
         partial[k] = grad[k * own_rank:(k + 1) * own_rank]
 

time: 24 us -> 24 us (level)
  no operation moved by 1% of the time
where the time goes in v7:
time: 24 us; the launch traced here: 23.8 us
  Pallas kernels  21.9 us (91%)
  local copies, waits for them, and re-layouts  1.27 us (5%)
  between operations  0.67 us (3%)
    pallas_call x1, Pallas kernels, per_device(): pl.pallas_call(functools.partial(kernel, sizes), out_shape=jax.ShapeDtype...  21.9 us
    unnamed x3, local copies, waits for them, and re-layouts  1.27 us

profile of v7, /device:TPU:0, one launch (start us, length us, event | category | flops | bytes accessed | tf_op | source)
XLA Modules:
  0.0 23.8 jit_solution(15679675447947764393)
XLA Ops:
  0.7 0.0 copy-start
  0.7 0.6 %copy-done = s32[4]{0:T(128)S(1)} copy-done((s32[4]{0:T(128)S(1)}, s32[4]{0:T(128)}, u32[]{:S(2)}) %copy-start) | copy-done | bytes 40
  1.3 21.9 %shard_map.64 = f32[2,4096]{1,0:T(2,128)S(1)} custom-call(s32[1]{0:T(128)S(6)} %copy.8.lengths_ref, s32[4]{0:T(128)S(1)} %copy-done, bf16[1,128,8192]{2,1,0:T(8,128)(2,1)} %hidden_ref.1, bf16[1,128,1024]{2,1,0:T(8,128)(2,1)} %cotangent_ref.1, bf16[16,8192]{1,0:T(8,128)(2,1)} %bitcast.1, bf16[4096,4096]{1,0:T(8,128)(2,1)} %projection_ref.1), custom_call_target="tpu_custom_call" | custom-call | tf_op jit(solution)/shard_map/pallas_call | solution.py:309
  23.2 0.6 %copy.9 = f32[2,4096]{1,0:T(2,128)} copy(f32[2,4096]{1,0:T(2,128)S(1)} %shard_map.64) | data formatting | bytes 65536
Async XLA Ops:
  0.7 0.7 %copy-start = (s32[4]{0:T(128)S(1)}, s32[4]{0:T(128)}, u32[]{:S(2)}) copy-start(s32[4]{0:T(128)} %order_ref.1) | copy-start | bytes 52

commit v8 on v5

--- a/solution.py
+++ b/solution.py
@@ -24,9 +24,9 @@
 
 def kernel(
     sizes,
-    lengths_ref, order_ref, hidden_ref, cotangent_ref, factor_ref, projection_ref,
+    numbers_ref, hidden_ref, cotangent_ref, factor_ref, projection_ref,
     out_ref,
-    lengths_v, order_v, hidden_v, cotangent_v, factor_v, projection_v,
+    numbers_v, hidden_v, cotangent_v, factor_v, projection_v,
     ids, partial, partial_in, grads, rows_out, rows_in, final_out, final_in, squares_in,
     local_sem, projection_sem, ids_send, ids_recv,
     grad_send, grad_recv, gather_send, gather_recv, rows_send, rows_recv,
@@ -63,10 +63,8 @@
 
     for k in range(HIDDEN_CHUNKS):
         hidden_copy(k).start()
-    order_copy = pltpu.make_async_copy(order_ref, order_v, local_sem.at[2])
-    order_copy.start()
-    lengths_copy = pltpu.make_async_copy(lengths_ref, lengths_v, local_sem.at[3])
-    lengths_copy.start()
+    numbers_copy = pltpu.make_async_copy(numbers_ref, numbers_v, local_sem.at[2])
+    numbers_copy.start()
     cotangent_copy = pltpu.make_async_copy(cotangent_ref.at[0], cotangent_v, local_sem.at[1])
     cotangent_copy.start()
 
@@ -101,23 +99,21 @@
     loop(1, ctx_count, greet_ctx)
     loop(1, slots, greet_slot)
 
-    order_copy.wait()
+    numbers_copy.wait()
     lane = lax.broadcasted_iota(jnp.int32, ids.shape[1:], 1)
     own_order = jnp.zeros(ids.shape[1:], jnp.int32)
     for i in range(group_slots):
-        own_order = jnp.where(lane == i, order_v[i], own_order)
+        own_order = jnp.where(lane == i, numbers_v[1 + i], own_order)
     ids[group] = own_order
 
-    lengths_copy.wait()
     factor_copy.wait()
-    hidden_copy(0).wait()
-    for k in range(chunk_count):
-        projection_copy(k).start()
-
     def add_down(k, down):
-        @pl.when(k > 0)
+        hidden_copy(k).wait()
+
+        @pl.when(k == HIDDEN_CHUNKS - 1)
         def _():
-            hidden_copy(k).wait()
+            for j in range(chunk_count):
+                projection_copy(j).start()
 
         columns = pl.ds(pl.multiple_of(k * step, LANES), step)
         return down + lax.dot_general(
@@ -127,7 +123,7 @@
 
     down = lax.fori_loop(0, HIDDEN_CHUNKS, add_down, jnp.zeros((rank, token_count), F32))
     position = ctx * token_count + lax.broadcasted_iota(jnp.int32, down.shape, 1)
-    down = jnp.where(position < lengths_v[0], down, 0.0).astype(BF16)
+    down = jnp.where(position < numbers_v[0], down, 0.0).astype(BF16)
     cotangent_copy.wait()
     grad = jnp.dot(down, cotangent_v[...], preferred_element_type=F32)
     for k in range(ctx_count):
@@ -259,8 +255,8 @@
         )
 
     square_sends = (feat_count - 1) * side_count
+    loop(1, side_count, lambda d: final_copy(d).start())
     loop(0, square_sends, lambda q: squares_copy(q).start())
-    loop(1, side_count, lambda d: final_copy(d).start())
     final_in[side] = final_out[side]
     loop(1, side_count, lambda d: final_copy(d, True).wait_recv())
     for x in range(side_count):
@@ -303,15 +299,15 @@
     block_lanes = max(LANES, own_rank * value_width // 16)
     block = -(-own_rank * value_width // block_lanes // 16) * 16
     assert example_count == 1 and depth == own_rank * value_width
+    numbers = jnp.concatenate([lengths, slot_example_order])
     dma = pltpu.SemaphoreType.DMA
     return pl.pallas_call(
         functools.partial(kernel, sizes),
         out_shape=jax.ShapeDtypeStruct((own_ids, columns), F32),
-        in_specs=[pl.BlockSpec(memory_space=pltpu.HBM)] * 6,
+        in_specs=[pl.BlockSpec(memory_space=pltpu.HBM)] * 5,
         out_specs=pl.BlockSpec(memory_space=pltpu.VMEM),
         scratch_shapes=[
-            pltpu.SMEM(lengths.shape, jnp.int32),
-            pltpu.SMEM(slot_example_order.shape, jnp.int32),
+            pltpu.SMEM(numbers.shape, jnp.int32),
             pltpu.VMEM((token_count, model_width), BF16),
             pltpu.VMEM((token_count, value_width), BF16),
             pltpu.VMEM((rank, model_width), BF16),
@@ -343,7 +339,7 @@
         compiler_params=pltpu.CompilerParams(
             collective_id=0, has_side_effects=True, vmem_limit_bytes=215 * 1024 * 256
         ),
-    )(lengths, slot_example_order, hidden, cotangent, adapter_down_factor.T, projection)
+    )(numbers, hidden, cotangent, adapter_down_factor.T, projection)
 
 
 def solution(mesh):

time: 24 us -> 24.1 us (level)
  other arithmetic: 0 us -> 0.73 us
  local copies, waits for them, and re-layouts: 1.27 us -> 0.62 us
    concatenate x0 -> x1, other arithmetic: none -> 0.73 us  [per_device(): numbers = jnp.concatenate([lengths, slot_example_order])]
    unnamed x3 -> x1, local copies, waits for them, and re-layouts: 1.27 us -> 0.62 us
where the time goes in v8:
time: 24.1 us; the launch traced here: 23.9 us
  Pallas kernels  21.9 us (91%)
  other arithmetic  0.73 us (3%)
  between operations  0.66 us (3%)
  local copies, waits for them, and re-layouts  0.62 us (3%)
    pallas_call x1, Pallas kernels, per_device(): pl.pallas_call(functools.partial(kernel, sizes), out_shape=jax.ShapeDtype...  21.9 us
    concatenate x1, other arithmetic, per_device(): numbers = jnp.concatenate([lengths, slot_example_order])  0.73 us
    unnamed x1, local copies, waits for them, and re-layouts  0.62 us

profile of v8, /device:TPU:0, one launch (start us, length us, event | category | flops | bytes accessed | tf_op | source)
XLA Modules:
  0.0 23.9 jit_solution(15374858183610137361)
XLA Ops:
  0.7 0.7 %pad_add_fusion.numbers_ref = s32[5]{0:T(128)S(1)} fusion(s32[4]{0:T(128)} %param.11, s32[1]{0:T(128)S(6)} %copy.8), kind=kLoop, calls=%fused_computation | loop fusion | flops 5 | bytes 40 | tf_op jit(solution)/shard_map/concatenate | solution.py:302
  1.4 21.9 %shard_map.64 = f32[2,4096]{1,0:T(2,128)S(1)} custom-call(s32[5]{0:T(128)S(1)} %pad_add_fusion.numbers_ref, bf16[1,128,8192]{2,1,0:T(8,128)(2,1)} %hidden_ref.1, bf16[1,128,1024]{2,1,0:T(8,128)(2,1)} %cotangent_ref.1, bf16[16,8192]{1,0:T(8,128)(2,1)} %bitcast.1, bf16[4096,4096]{1,0:T(8,128)(2,1)} %projection_ref.1), custom_call_target="tpu_custom_call" | custom-call | tf_op jit(solution)/shard_map/pallas_call | solution.py:304
  23.3 0.6 %copy.9 = f32[2,4096]{1,0:T(2,128)} copy(f32[2,4096]{1,0:T(2,128)S(1)} %shard_map.64) | data formatting | bytes 65536

commit v9 on v5

--- a/solution.py
+++ b/solution.py
@@ -27,7 +27,7 @@
     lengths_ref, order_ref, hidden_ref, cotangent_ref, factor_ref, projection_ref,
     out_ref,
     lengths_v, order_v, hidden_v, cotangent_v, factor_v, projection_v,
-    ids, partial, partial_in, grads, rows_out, rows_in, final_out, final_in, squares_in,
+    ids, own_partial, partial, partial_in, grads, rows_out, rows_in, final_out, final_in, squares_in,
     local_sem, projection_sem, ids_send, ids_recv,
     grad_send, grad_recv, gather_send, gather_recv, rows_send, rows_recv,
     final_send, final_recv, squares_send, squares_recv,
@@ -131,7 +131,14 @@
     cotangent_copy.wait()
     grad = jnp.dot(down, cotangent_v[...], preferred_element_type=F32)
     for k in range(ctx_count):
-        partial[k] = grad[k * own_rank:(k + 1) * own_rank]
+        rows = [
+            grad[k * own_rank:(k + 1) * own_rank, q * block_lanes:(q + 1) * block_lanes]
+            for q in range(pieces)
+        ]
+        if pieces * own_rank < block:
+            rows.append(jnp.zeros((block - pieces * own_rank, block_lanes), F32))
+        own_partial[k] = jnp.concatenate(rows, axis=0)
+        partial[k] = own_partial[k].astype(BF16)
 
     pl.semaphore_wait(barrier, ctx_count - 1 + slots - 1)
 
@@ -155,7 +162,6 @@
 
     loop(1, ctx_count, lambda d: grad_copy(d).start())
     loop(1, group_count, lambda d: ids_copy(d).start())
-    partial_in[ctx] = partial[ctx]
 
     loop(1, group_count, lambda d: ids_copy(d, True).wait_recv())
     pick_shape = (own_rank * pieces * padded, slots * block)
@@ -172,13 +178,10 @@
     pick = pick.astype(F32).astype(BF16)
 
     loop(1, ctx_count, lambda d: grad_copy(d, True).wait_recv())
-    total = partial_in[0]
-    for k in range(1, ctx_count):
-        total += partial_in[k]
-    rows = [total[:, q * block_lanes:(q + 1) * block_lanes] for q in range(pieces)]
-    if pieces * own_rank < block:
-        rows.append(jnp.zeros((block - pieces * own_rank, block_lanes), F32))
-    grads[slot] = jnp.concatenate(rows, axis=0).astype(BF16)
+    total = own_partial[ctx]
+    for d in range(1, ctx_count):
+        total += partial_in[ctx_peer(d)].astype(F32)
+    grads[slot] = total.astype(BF16)
 
     def gather_copy(d, landing=None):
         other, device = slot_peer(d)
@@ -259,8 +262,8 @@
         )
 
     square_sends = (feat_count - 1) * side_count
+    loop(1, side_count, lambda d: final_copy(d).start())
     loop(0, square_sends, lambda q: squares_copy(q).start())
-    loop(1, side_count, lambda d: final_copy(d).start())
     final_in[side] = final_out[side]
     loop(1, side_count, lambda d: final_copy(d, True).wait_recv())
     for x in range(side_count):
@@ -317,8 +320,9 @@
             pltpu.VMEM((rank, model_width), BF16),
             pltpu.VMEM((chunk_count, depth, chunk), BF16),
             pltpu.VMEM((group_count, 8, LANES), jnp.int32),
-            pltpu.VMEM((ctx_count, own_rank, value_width), F32),
-            pltpu.VMEM((ctx_count, own_rank, value_width), F32),
+            pltpu.VMEM((ctx_count, block, block_lanes), F32),
+            pltpu.VMEM((ctx_count, block, block_lanes), BF16),
+            pltpu.VMEM((ctx_count, block, block_lanes), BF16),
             pltpu.VMEM((slots, block, block_lanes), BF16),
             pltpu.VMEM((chunk_count, slots * chunk // LANES, LANES), BF16),
             pltpu.VMEM((ctx_count, chunk_count, slots * chunk // LANES, LANES), BF16),

time: 24 us -> 23.7 us (0.987)
  Pallas kernels: 21.9 us -> 21.6 us
    pallas_call x1, Pallas kernels: 21.9 us -> 21.6 us  [per_device(): pl.pallas_call(functools.partial(kernel, sizes), out_shape=jax.ShapeDtype...]
where the time goes in v9:
time: 23.7 us; the launch traced here: 23.6 us
  Pallas kernels  21.6 us (91%)
  local copies, waits for them, and re-layouts  1.27 us (5%)
  between operations  0.67 us (3%)
    pallas_call x1, Pallas kernels, per_device(): pl.pallas_call(functools.partial(kernel, sizes), out_shape=jax.ShapeDtype...  21.6 us
    unnamed x3, local copies, waits for them, and re-layouts  1.27 us

profile of v9, /device:TPU:0, one launch (start us, length us, event | category | flops | bytes accessed | tf_op | source)
XLA Modules:
  0.0 23.6 jit_solution(11125199322697897933)
XLA Ops:
  0.7 0.0 copy-start
  0.7 0.6 %copy-done = s32[4]{0:T(128)S(1)} copy-done((s32[4]{0:T(128)S(1)}, s32[4]{0:T(128)}, u32[]{:S(2)}) %copy-start) | copy-done | bytes 40
  1.3 21.6 %shard_map.64 = f32[2,4096]{1,0:T(2,128)S(1)} custom-call(s32[1]{0:T(128)S(6)} %copy.8.lengths_ref, s32[4]{0:T(128)S(1)} %copy-done, bf16[1,128,8192]{2,1,0:T(8,128)(2,1)} %hidden_ref.1, bf16[1,128,1024]{2,1,0:T(8,128)(2,1)} %cotangent_ref.1, bf16[16,8192]{1,0:T(8,128)(2,1)} %bitcast.1, bf16[4096,4096]{1,0:T(8,128)(2,1)} %projection_ref.1), custom_call_target="tpu_custom_call" | custom-call | tf_op jit(solution)/shard_map/pallas_call | solution.py:310
  22.9 0.6 %copy.9 = f32[2,4096]{1,0:T(2,128)} copy(f32[2,4096]{1,0:T(2,128)S(1)} %shard_map.64) | data formatting | bytes 65536
Async XLA Ops:
  0.7 0.7 %copy-start = (s32[4]{0:T(128)S(1)}, s32[4]{0:T(128)}, u32[]{:S(2)}) copy-start(s32[4]{0:T(128)} %order_ref.1) | copy-start | bytes 52

commit v10 on v5

--- a/solution.py
+++ b/solution.py
@@ -12,6 +12,7 @@
 BF16 = jnp.bfloat16
 LANES = 128
 HIDDEN_CHUNKS = 4
+PROJECTION_CHUNKS = 4
 
 
 def loop(low, high, body):
@@ -43,8 +44,9 @@
     token_count, model_width = hidden_v.shape
     rank = factor_v.shape[0]
     own_rank = rank // ctx_count
-    chunk_count, depth, chunk = projection_v.shape
-    width = chunk_count * chunk
+    depth, width = projection_v.shape
+    chunk_count = rows_out.shape[0]
+    chunk = width // chunk_count
     value_width = cotangent_v.shape[1]
     padded = max(8, slots)
     own_ids = out_ref.shape[0]
@@ -71,9 +73,10 @@
     cotangent_copy.start()
 
     def projection_copy(k):
-        columns = pl.ds(pl.multiple_of(side * width + k * chunk, LANES), chunk)
+        rows = pl.ds(k * (depth // PROJECTION_CHUNKS), depth // PROJECTION_CHUNKS)
+        columns = pl.ds(pl.multiple_of(side * width, LANES), width)
         return pltpu.make_async_copy(
-            projection_ref.at[:, columns], projection_v.at[k], projection_sem.at[k]
+            projection_ref.at[rows, columns], projection_v.at[rows], projection_sem.at[k]
         )
 
     def at_side(x):
@@ -111,7 +114,7 @@
     lengths_copy.wait()
     factor_copy.wait()
     hidden_copy(0).wait()
-    for k in range(chunk_count):
+    for k in range(PROJECTION_CHUNKS):
         projection_copy(k).start()
 
     def add_down(k, down):
@@ -205,11 +208,11 @@
         )
 
     def project(k, carry):
-        projection_copy(k).wait()
+        columns = pl.ds(pl.multiple_of(k * chunk, LANES), chunk)
         product = jnp.zeros((padded, chunk), F32)
         for i in range(own_rank * pieces):
             product += jnp.dot(
-                left[i], projection_v[k, i * block_lanes:(i + 1) * block_lanes, :],
+                left[i], projection_v[i * block_lanes:(i + 1) * block_lanes, columns],
                 preferred_element_type=F32,
             )
         lanes = [product[:slots, p * LANES:(p + 1) * LANES] for p in range(chunk // LANES)]
@@ -219,6 +222,8 @@
         rows_in[ctx, k] = rows_out[k]
         return carry
 
+    for k in range(PROJECTION_CHUNKS):
+        projection_copy(k).wait()
     lax.fori_loop(0, chunk_count, project, 0)
 
     for k in range(chunk_count):
@@ -315,7 +320,7 @@
             pltpu.VMEM((token_count, model_width), BF16),
             pltpu.VMEM((token_count, value_width), BF16),
             pltpu.VMEM((rank, model_width), BF16),
-            pltpu.VMEM((chunk_count, depth, chunk), BF16),
+            pltpu.VMEM((depth, width), BF16),
             pltpu.VMEM((group_count, 8, LANES), jnp.int32),
             pltpu.VMEM((ctx_count, own_rank, value_width), F32),
             pltpu.VMEM((ctx_count, own_rank, value_width), F32),
@@ -326,7 +331,7 @@
             pltpu.VMEM((side_count, chunk_count * own_ids, chunk + LANES), F32),
             pltpu.VMEM((slots, chunk_count * own_ids, LANES), F32),
             dma((4 + HIDDEN_CHUNKS,)),
-            dma((chunk_count,)),
+            dma((PROJECTION_CHUNKS,)),
             dma((group_count,)),
             dma((group_count,)),
             dma((ctx_count,)),

time: 24 us -> 24 us (level)
  no operation moved by 1% of the time
where the time goes in v10:
time: 24 us; the launch traced here: 23.8 us
  Pallas kernels  21.9 us (91%)
  local copies, waits for them, and re-layouts  1.27 us (5%)
  between operations  0.67 us (3%)
    pallas_call x1, Pallas kernels, per_device(): pl.pallas_call(functools.partial(kernel, sizes), out_shape=jax.ShapeDtype...  21.9 us
    unnamed x3, local copies, waits for them, and re-layouts  1.27 us

profile of v10, /device:TPU:0, one launch (start us, length us, event | category | flops | bytes accessed | tf_op | source)
XLA Modules:
  0.0 23.8 jit_solution(12760241081141328550)
XLA Ops:
  0.7 0.0 copy-start
  0.7 0.6 %copy-done = s32[4]{0:T(128)S(1)} copy-done((s32[4]{0:T(128)S(1)}, s32[4]{0:T(128)}, u32[]{:S(2)}) %copy-start) | copy-done | bytes 40
  1.3 21.9 %shard_map.64 = f32[2,4096]{1,0:T(2,128)S(1)} custom-call(s32[1]{0:T(128)S(6)} %copy.8.lengths_ref, s32[4]{0:T(128)S(1)} %copy-done, bf16[1,128,8192]{2,1,0:T(8,128)(2,1)} %hidden_ref.1, bf16[1,128,1024]{2,1,0:T(8,128)(2,1)} %cotangent_ref.1, bf16[16,8192]{1,0:T(8,128)(2,1)} %bitcast.1, bf16[4096,4096]{1,0:T(8,128)(2,1)} %projection_ref.1), custom_call_target="tpu_custom_call" | custom-call | tf_op jit(solution)/shard_map/pallas_call | solution.py:312
  23.2 0.6 %copy.9 = f32[2,4096]{1,0:T(2,128)} copy(f32[2,4096]{1,0:T(2,128)S(1)} %shard_map.64) | data formatting | bytes 65536
Async XLA Ops:
  0.7 0.7 %copy-start = (s32[4]{0:T(128)S(1)}, s32[4]{0:T(128)}, u32[]{:S(2)}) copy-start(s32[4]{0:T(128)} %order_ref.1) | copy-start | bytes 52

commit v11 on v5

--- a/solution.py
+++ b/solution.py
@@ -51,6 +51,31 @@
     block, block_lanes = grads.shape[1:]
     pieces = value_width // block_lanes
 
+    def at_side(x):
+        return {"group": x // ex_count, "ex": lax.rem(x, ex_count)}
+
+    def ctx_peer(d):
+        return lax.rem(ctx + d, ctx_count)
+
+    def slot_peer(d):
+        other = lax.rem(slot + d, slots)
+        return other, {"feat": other // side_count, **at_side(lax.rem(other, side_count))}
+
+    barrier = pltpu.get_barrier_semaphore()
+
+    def greet_ctx(d):
+        pl.semaphore_signal(
+            barrier, inc=1, device_id_type=MESH, device_id={"ctx": ctx_peer(d)}
+        )
+
+    def greet_slot(d):
+        pl.semaphore_signal(
+            barrier, inc=1, device_id_type=MESH, device_id=slot_peer(d)[1]
+        )
+
+    loop(1, ctx_count, greet_ctx)
+    loop(1, slots, greet_slot)
+
     step = model_width // HIDDEN_CHUNKS
     factor_copy = pltpu.make_async_copy(factor_ref, factor_v, local_sem.at[0])
     factor_copy.start()
@@ -75,31 +100,6 @@
         return pltpu.make_async_copy(
             projection_ref.at[:, columns], projection_v.at[k], projection_sem.at[k]
         )
-
-    def at_side(x):
-        return {"group": x // ex_count, "ex": lax.rem(x, ex_count)}
-
-    def ctx_peer(d):
-        return lax.rem(ctx + d, ctx_count)
-
-    def slot_peer(d):
-        other = lax.rem(slot + d, slots)
-        return other, {"feat": other // side_count, **at_side(lax.rem(other, side_count))}
-
-    barrier = pltpu.get_barrier_semaphore()
-
-    def greet_ctx(d):
-        pl.semaphore_signal(
-            barrier, inc=1, device_id_type=MESH, device_id={"ctx": ctx_peer(d)}
-        )
-
-    def greet_slot(d):
-        pl.semaphore_signal(
-            barrier, inc=1, device_id_type=MESH, device_id=slot_peer(d)[1]
-        )
-
-    loop(1, ctx_count, greet_ctx)
-    loop(1, slots, greet_slot)
 
     order_copy.wait()
     lane = lax.broadcasted_iota(jnp.int32, ids.shape[1:], 1)
@@ -259,8 +259,8 @@
         )
 
     square_sends = (feat_count - 1) * side_count
+    loop(1, side_count, lambda d: final_copy(d).start())
     loop(0, square_sends, lambda q: squares_copy(q).start())
-    loop(1, side_count, lambda d: final_copy(d).start())
     final_in[side] = final_out[side]
     loop(1, side_count, lambda d: final_copy(d, True).wait_recv())
     for x in range(side_count):

time: 24 us -> 24 us (level)
  no operation moved by 1% of the time
where the time goes in v11:
time: 24 us; the launch traced here: 23.8 us
  Pallas kernels  21.9 us (91%)
  local copies, waits for them, and re-layouts  1.27 us (5%)
  between operations  0.67 us (3%)
    pallas_call x1, Pallas kernels, per_device(): pl.pallas_call(functools.partial(kernel, sizes), out_shape=jax.ShapeDtype...  21.9 us
    unnamed x3, local copies, waits for them, and re-layouts  1.27 us

profile of v11, /device:TPU:0, one launch (start us, length us, event | category | flops | bytes accessed | tf_op | source)
XLA Modules:
  0.0 23.8 jit_solution(4313912190626861491)
XLA Ops:
  0.7 0.0 copy-start
  0.7 0.6 %copy-done = s32[4]{0:T(128)S(1)} copy-done((s32[4]{0:T(128)S(1)}, s32[4]{0:T(128)}, u32[]{:S(2)}) %copy-start) | copy-done | bytes 40
  1.3 21.9 %shard_map.64 = f32[2,4096]{1,0:T(2,128)S(1)} custom-call(s32[1]{0:T(128)S(6)} %copy.8.lengths_ref, s32[4]{0:T(128)S(1)} %copy-done, bf16[1,128,8192]{2,1,0:T(8,128)(2,1)} %hidden_ref.1, bf16[1,128,1024]{2,1,0:T(8,128)(2,1)} %cotangent_ref.1, bf16[16,8192]{1,0:T(8,128)(2,1)} %bitcast.1, bf16[4096,4096]{1,0:T(8,128)(2,1)} %projection_ref.1), custom_call_target="tpu_custom_call" | custom-call | tf_op jit(solution)/shard_map/pallas_call | solution.py:307
  23.2 0.6 %copy.9 = f32[2,4096]{1,0:T(2,128)} copy(f32[2,4096]{1,0:T(2,128)S(1)} %shard_map.64) | data formatting | bytes 65536
Async XLA Ops:
  0.7 0.7 %copy-start = (s32[4]{0:T(128)S(1)}, s32[4]{0:T(128)}, u32[]{:S(2)}) copy-start(s32[4]{0:T(128)} %order_ref.1) | copy-start | bytes 52
